TPU v7x, 32 devices: a whole 2x2x4 slice. The times are simulated.
32 devices in a mesh: dp: 16 (over z, y, x), tensor: 2 (over core).
Axes of the slice: x: 2, y: 2, z: 4, core: 2. Of those that a mesh axis runs over, the one named last changes fastest.
Arguments:
- tokens: bfloat16 [4096, 8192], P('dp', 'tensor'), may hold values from -6 to 6
- norm_gain: bfloat16 [8192], P('tensor'), may hold values from 0.099609375 to 1.8984375
- kept_blocks: bfloat16 [8192, 6144], P('dp', 'tensor'), may hold values from -0.09375 to 0.09375
- block_cols: int32 [64, 48], P('dp', 'tensor'), may hold values from 0 to 39, as said below
- row_counts: int32 [64, 2], P('dp', 'tensor'), may hold values from 16 to 24, as said below
Outputs:
- projected: bfloat16 [4096, 10240], P('dp', 'tensor')
Inputs may be any that keep to these rules, and one draw needn't show every extreme that they name: `block_cols`: in each row block the 24 slots of one shard name distinct column blocks of that shard, also the slots beyond row_counts. `row_counts`: in every shard some row block has 24 kept blocks.
All inputs are finite; a program needn't handle non-finite values.
Results may differ from a plain program's by a relative error of at most 0.0049.
Values may be sent and summed in bfloat16 or wider, within the bound.
A program may use at most 128 MiB of HBM per device.

v0:
```python
import math

import jax
import jax.numpy as jnp
from jax import lax
from jax.sharding import PartitionSpec as P

KVH = 8
GROUP = 8
HD = 128
BS = 128


rope_theta = 500000.0


def rotate(mixed, positions):
    row_count = mixed.shape[0]
    head_view = mixed.reshape(row_count, -1, GROUP + 2, HD)
    half_size = HD // 2
    inverse_freq = rope_theta ** (-(jnp.arange(half_size).astype(jnp.float32) * 2.0 / HD))
    angles = positions[:, None] * inverse_freq[None, :]
    cosine = jnp.cos(angles)[:, None, None, :]
    sine_part = jnp.sin(angles)[:, None, None, :]
    first_half = head_view[..., :half_size]
    second = head_view[..., half_size:]
    turned = jnp.concatenate(
        [first_half * cosine - second * sine_part, second * cosine + first_half * sine_part],
        axis=-1,
    )
    rotated_heads = (jnp.arange(GROUP + 2) < GROUP + 1)[None, None, :, None]
    return jnp.where(rotated_heads, turned, head_view).reshape(row_count, -1)


def per_device(tokens, norm_gain, kept_blocks, block_cols, row_counts):
    tensor_count = lax.axis_size("tensor")
    column_blocks = KVH // tensor_count * (GROUP + 2) * HD // BS
    rows_here = block_cols.shape[0]
    slot_count = block_cols.shape[1]
    gathered, gain_all = (
        lax.all_gather(tokens, "tensor", axis=1, tiled=True),
        lax.all_gather(norm_gain, "tensor", axis=0, tiled=True),
    )
    floats = gathered.astype(jnp.float32)
    mean_square = jnp.mean(floats * floats, axis=-1, keepdims=True)
    normed = (floats * lax.rsqrt(mean_square + 1e-05) * gain_all.astype(jnp.float32)).astype(
        jnp.bfloat16
    )
    filled = jnp.arange(slot_count)[None, :] < row_counts
    placing = (
        (block_cols[:, :, None] == jnp.arange(column_blocks)[None, None, :]) & filled[:, :, None]
    ).astype(jnp.bfloat16)
    stacked = kept_blocks.reshape(rows_here, BS, slot_count * BS)
    initial = jnp.zeros((tokens.shape[0], column_blocks * BS), jnp.float32)
    summed = initial
    block_piece = lax.all_gather(stacked, "dp", axis=0, tiled=True)
    place_piece = lax.all_gather(placing, "dp", axis=0, tiled=True)
    piece_rows = block_piece.shape[0]
    group_size = math.gcd(piece_rows, 8)
    step_count = piece_rows // group_size
    block_groups = block_piece.reshape(step_count, group_size, BS, slot_count * BS)
    place_groups = place_piece.reshape(step_count, group_size, slot_count, column_blocks)

    def advance(running, step_input):
        step_index, block_set, place_set = step_input
        feature_rows = lax.dynamic_slice_in_dim(
            normed, step_index * group_size * BS, group_size * BS, 1
        )
        dense_rows = jnp.einsum(
            "gksj,gsc->gkcj",
            block_set.reshape(group_size, BS, slot_count, BS),
            place_set,
            preferred_element_type=jnp.float32,
        )
        dense_rows = dense_rows.astype(jnp.bfloat16).reshape(group_size * BS, column_blocks * BS)
        return (
            running + jnp.dot(feature_rows, dense_rows, preferred_element_type=jnp.float32),
            None,
        )

    summed, _ = lax.scan(
        advance, summed, (jnp.arange(step_count, dtype=jnp.int32), block_groups, place_groups)
    )
    positions = jnp.arange(tokens.shape[0]).astype(jnp.float32)
    return rotate(summed, positions).astype(jnp.bfloat16)


def solution(mesh):
    in_specs = (
        P("dp", "tensor"),
        P("tensor"),
        P("dp", "tensor"),
        P("dp", "tensor"),
        P("dp", "tensor"),
    )
    out_specs = P("dp", "tensor")
    return jax.shard_map(
        per_device, mesh=mesh, in_specs=in_specs, out_specs=out_specs, check_vma=False
    )
```

profile of v0, /device:TPU:0, one launch (start us, length us, event | category | flops | bytes accessed | tf_op | source)
XLA Modules:
  0.0 755.7 jit_solution(8645023875587397462)
XLA Ops:
  6.5 0.0 all-gather.3.cloned.1.call-start
  6.5 0.7 all-gather.3.cloned.1.call-update
  7.3 0.0 all-gather.5.cloned.1.call-start
  7.3 0.7 all-gather.5.cloned.1.call-update
  8.0 1.9 all_gather.13
  10.0 0.1 broadcast_in_dim.11
  10.1 0.1 iota_compare_fusion.1
  10.2 0.0 copy-done.4
  10.2 0.1 fusion.21
  10.3 45.7 %all_gather.14 = bf16[64,24,40]{2,1,0:T(8,128)(2,1)S(1)} all-gather(bf16[4,24,40]{2,1,0:T(8,128)(2,1)S(1)} %fusion.21), channel_id=1, replica_groups=mesh['dp'=16,'tensor'=2] {'dp'}, dimensions={0}, use_global_device_ids=true | all-gather | bytes 130560 | tf_op jit(solution)/shard_map/all_gather | solution.py:57
  56.0 1.0 multiply_cosine_fusion
  57.0 3.3 fusion.16
  60.3 0.2 copy-done
  60.5 3.2 fusion.18
  63.7 475.7 %all-gather.5.cloned.1.call-done = bf16[64,128,3072]{2,1,0:T(8,128)(2,1)} async-done(((bf16[4,128,3072]{2,1,0:T(8,128)(2,1)}), bf16[64,128,3072]{2,1,0:T(8,128)(2,1)}) %all-gather.5.cloned.1.call-update) | async-done | bytes 50331664 | tf_op jit(solution)/shard_map/all_gather | solution.py:56
  539.3 194.1 %while.13 = (s32[]{:T(128)}, f32[256,5120]{1,0:T(8,128)}, s32[8]{0:T(128)S(1)}, bf16[256,8192]{1,0:T(8,128)(2,1)}, bf16[8,8,24,40]{3,2,1,0:T(8,128)(2,1)S(1)}, /...) while((s32[]{:T(128)}, f32[256,5120]{1,0:T(8,128)}, ...), condition=%wide.region_2.3_spmd.clone, body=%wide.region_1.2_spmd.clone.sunk | while | flops 2943877120 | bytes 63488176 | solution.py:81
  539.3 0.6 dynamic_slice.45
  540.6 3.2 constant_dynamic-slice_fusion.2
  543.9 1.9 copy.24
  545.8 7.1 fusion.30
  552.9 9.4 %fusion.31 = f32[256,5120]{1,0:T(8,128)} fusion(bf16[128,8,40,128]{3,2,1,0:T(8,128)(2,1)} %bitcast.49, f32[256,5120]{1,0:T(8,128)} %get-tuple-element.168, pred[]{:T(512)S(6)} %compare.3, bf16[256,8192]{1,0:T(8,128)(2,1)} %get-tuple-element.180, s32[]{:T(128)S(6)} %select_n.17), kind=kOutput, calls=%fused_computation.3.clone.1 | convolution fusion | flops 2686976000 | bytes 21495812 | tf_op jit(solution)/shard_map/while/body/eval_jaxpr/dot_general | solution.py:77
  562.3 0.6 dynamic_slice.45
  563.6 3.2 constant_dynamic-slice_fusion.2
  566.8 1.9 copy.24
  568.7 7.1 fusion.30
  575.9 10.9 %fusion.31 = f32[256,5120]{1,0:T(8,128)} fusion(bf16[128,8,40,128]{3,2,1,0:T(8,128)(2,1)} %bitcast.49, f32[256,5120]{1,0:T(8,128)} %get-tuple-element.168, pred[]{:T(512)S(6)} %compare.3, bf16[256,8192]{1,0:T(8,128)(2,1)} %get-tuple-element.180, s32[]{:T(128)S(6)} %select_n.17), kind=kOutput, calls=%fused_computation.3.clone.1 | convolution fusion | flops 2686976000 | bytes 21495812 | tf_op jit(solution)/shard_map/while/body/eval_jaxpr/dot_general | solution.py:77
  586.7 0.6 dynamic_slice.45
  588.0 3.2 constant_dynamic-slice_fusion.2
  591.3 1.9 copy.24
  593.2 7.1 fusion.30
  600.3 10.9 %fusion.31 = f32[256,5120]{1,0:T(8,128)} fusion(bf16[128,8,40,128]{3,2,1,0:T(8,128)(2,1)} %bitcast.49, f32[256,5120]{1,0:T(8,128)} %get-tuple-element.168, pred[]{:T(512)S(6)} %compare.3, bf16[256,8192]{1,0:T(8,128)(2,1)} %get-tuple-element.180, s32[]{:T(128)S(6)} %select_n.17), kind=kOutput, calls=%fused_computation.3.clone.1 | convolution fusion | flops 2686976000 | bytes 21495812 | tf_op jit(solution)/shard_map/while/body/eval_jaxpr/dot_general | solution.py:77
  611.2 0.6 dynamic_slice.45
  612.5 3.2 constant_dynamic-slice_fusion.2
  615.7 1.9 copy.24
  617.6 7.1 fusion.30
  624.8 10.9 %fusion.31 = f32[256,5120]{1,0:T(8,128)} fusion(bf16[128,8,40,128]{3,2,1,0:T(8,128)(2,1)} %bitcast.49, f32[256,5120]{1,0:T(8,128)} %get-tuple-element.168, pred[]{:T(512)S(6)} %compare.3, bf16[256,8192]{1,0:T(8,128)(2,1)} %get-tuple-element.180, s32[]{:T(128)S(6)} %select_n.17), kind=kOutput, calls=%fused_computation.3.clone.1 | convolution fusion | flops 2686976000 | bytes 21495812 | tf_op jit(solution)/shard_map/while/body/eval_jaxpr/dot_general | solution.py:77
  635.6 0.6 dynamic_slice.45
  636.9 3.2 constant_dynamic-slice_fusion.2
  640.2 1.9 copy.24
  642.1 7.1 fusion.30
  649.2 10.9 %fusion.31 = f32[256,5120]{1,0:T(8,128)} fusion(bf16[128,8,40,128]{3,2,1,0:T(8,128)(2,1)} %bitcast.49, f32[256,5120]{1,0:T(8,128)} %get-tuple-element.168, pred[]{:T(512)S(6)} %compare.3, bf16[256,8192]{1,0:T(8,128)(2,1)} %get-tuple-element.180, s32[]{:T(128)S(6)} %select_n.17), kind=kOutput, calls=%fused_computation.3.clone.1 | convolution fusion | flops 2686976000 | bytes 21495812 | tf_op jit(solution)/shard_map/while/body/eval_jaxpr/dot_general | solution.py:77
  660.1 0.6 dynamic_slice.45
  661.4 3.2 constant_dynamic-slice_fusion.2
  664.6 1.9 copy.24
  666.5 7.1 fusion.30
  673.7 10.9 %fusion.31 = f32[256,5120]{1,0:T(8,128)} fusion(bf16[128,8,40,128]{3,2,1,0:T(8,128)(2,1)} %bitcast.49, f32[256,5120]{1,0:T(8,128)} %get-tuple-element.168, pred[]{:T(512)S(6)} %compare.3, bf16[256,8192]{1,0:T(8,128)(2,1)} %get-tuple-element.180, s32[]{:T(128)S(6)} %select_n.17), kind=kOutput, calls=%fused_computation.3.clone.1 | convolution fusion | flops 2686976000 | bytes 21495812 | tf_op jit(solution)/shard_map/while/body/eval_jaxpr/dot_general | solution.py:77
  684.5 0.6 dynamic_slice.45
  685.8 3.2 constant_dynamic-slice_fusion.2
  689.1 1.9 copy.24
  691.0 7.1 fusion.30
  698.1 10.9 %fusion.31 = f32[256,5120]{1,0:T(8,128)} fusion(bf16[128,8,40,128]{3,2,1,0:T(8,128)(2,1)} %bitcast.49, f32[256,5120]{1,0:T(8,128)} %get-tuple-element.168, pred[]{:T(512)S(6)} %compare.3, bf16[256,8192]{1,0:T(8,128)(2,1)} %get-tuple-element.180, s32[]{:T(128)S(6)} %select_n.17), kind=kOutput, calls=%fused_computation.3.clone.1 | convolution fusion | flops 2686976000 | bytes 21495812 | tf_op jit(solution)/shard_map/while/body/eval_jaxpr/dot_general | solution.py:77
  709.0 0.6 dynamic_slice.45
  710.3 3.2 constant_dynamic-slice_fusion.2
  713.5 1.9 copy.24
  715.4 7.1 fusion.30
  722.6 10.9 %fusion.31 = f32[256,5120]{1,0:T(8,128)} fusion(bf16[128,8,40,128]{3,2,1,0:T(8,128)(2,1)} %bitcast.49, f32[256,5120]{1,0:T(8,128)} %get-tuple-element.168, pred[]{:T(512)S(6)} %compare.3, bf16[256,8192]{1,0:T(8,128)(2,1)} %get-tuple-element.180, s32[]{:T(128)S(6)} %select_n.17), kind=kOutput, calls=%fused_computation.3.clone.1 | convolution fusion | flops 2686976000 | bytes 21495812 | tf_op jit(solution)/shard_map/while/body/eval_jaxpr/dot_general | solution.py:77
  733.4 5.9 copy.9
  739.4 0.0 copy-done.1
  739.4 0.0 slice-start.1
  739.4 3.5 multiply_subtract_fusion
  743.0 0.3 pad_maximum_fusion
  743.3 0.2 slice-done.1
  743.4 2.6 fusion.19
  746.1 2.8 copy.11
  (21 shorter events, 0.1 us)
Async XLA Ops:
  6.5 1.5 copy-start.3
  6.5 3.5 copy-start.5
  6.5 3.6 copy-start.4
  6.5 50.4 %all-gather.3.cloned.1.call-start = ((), (), s32[]{:S(2)}) async-start(), calls=%async_computation | async-start | bytes 6291456 | tf_op jit(solution)/shard_map/all_gather | solution.py:41
  7.3 532.1 %all-gather.5.cloned.1.call-start = ((), (), s32[]{:S(2)}) async-start(), calls=%async_computation.1 | async-start | bytes 53477376 | tf_op jit(solution)/shard_map/all_gather | solution.py:56
  57.0 3.5 copy-start
  733.4 6.0 copy-start.1
  733.4 6.0 copy-start.2
  739.4 3.9 slice-start
  739.4 4.0 slice-start.1
Sparse Core Ops, SparseCore 0:
  8.9 16.3 all-gather.2
  28.1 511.1 all-gather.4
where the time goes:
time: 756 us
  waiting for transfers between devices  477 us (63%)
  matrix products  142 us (19%)
  local copies, waits for them, and re-layouts  55.6 us (7%)
  blocking collectives  47.7 us (6%)
  other arithmetic  14.1 us (2%)
  between operations  13.5 us (2%)
    all_gather x1, waiting for transfers between devices, per_device(): block_piece = lax.all_gather(stacked, 'dp', axis=0, tiled=True)  476 us
    dot_general x8, matrix products, advance(): jnp.dot(feature_rows, dense_rows, preferred_element_type=jnp.float32)  85.5 us
    dot_general x8, matrix products, advance(): jnp.einsum('gksj,gsc->gkcj', block_set.reshape(group_size, BS, slot_count...  57 us
    all_gather x1, blocking collectives, per_device(): place_piece = lax.all_gather(placing, 'dp', axis=0, tiled=True)  45.7 us
    dynamic_slice x16, local copies, waits for them, and re-layouts, per_device(): lax.scan(advance, summed, (jnp.arange(step_count, dtype=jnp.int32), block...  31.1 us
    while x8, local copies, waits for them, and re-layouts  15.4 us
  transfers between devices with their start and end apart: 2, of which 1 were waited for; matrix products, arithmetic and copies ran while one was open for 1% of the time, Pallas kernels for 0%

commit v1 on v0

v1 whole, which is shorter than its diff:
```python
import functools

import jax
import jax.numpy as jnp
from jax import lax
from jax.experimental import pallas as pl
from jax.experimental.pallas import tpu as pltpu
from jax.sharding import PartitionSpec as P

KVH = 8
GROUP = 8
HD = 128
BS = 128


rope_theta = 500000.0


def rotate(mixed, positions):
    row_count = mixed.shape[0]
    head_view = mixed.reshape(row_count, -1, HD)
    heads = head_view.shape[1]
    half_size = HD // 2
    inverse_freq = rope_theta ** (-(jnp.arange(half_size).astype(jnp.float32) * 2.0 / HD))
    angles = positions[:, None] * inverse_freq[None, :]
    cosine = jnp.cos(angles)
    sine_part = jnp.sin(angles)
    cos_full = jnp.concatenate([cosine, cosine], axis=-1)[:, None, :]
    sin_full = jnp.concatenate([-sine_part, sine_part], axis=-1)[:, None, :]
    swapped = jnp.roll(head_view, half_size, axis=-1)
    turned = head_view * cos_full + swapped * sin_full
    rotated_heads = (jnp.arange(heads) % (GROUP + 2) < GROUP + 1)[None, :, None]
    return jnp.where(rotated_heads, turned, head_view).reshape(row_count, -1)


def place_body(where_ref, blocks_ref, *rest, slots, column_blocks):
    out_ref = rest[-1]
    row = pl.program_id(0)
    for column in range(column_blocks):
        slot = where_ref[1 + row * column_blocks + column]
        start = pl.multiple_of(jnp.minimum(slot, slots - 1) * BS, BS)
        block = blocks_ref[:, pl.ds(start, BS)]
        out_ref[:, column * BS : (column + 1) * BS] = jnp.where(
            slot < slots, block, jnp.zeros_like(block)
        )


def place(where, blocks, dense, total_rows, column_blocks):
    rows, width = blocks.shape
    slots = width // BS
    in_specs = [pl.BlockSpec((BS, width), lambda r, where: (r, 0))]
    operands = [where, blocks]
    aliases = {}
    if dense is not None:
        in_specs.append(pl.BlockSpec(memory_space=pl.ANY))
        operands.append(dense)
        aliases = {2: 0}
    return pl.pallas_call(
        functools.partial(place_body, slots=slots, column_blocks=column_blocks),
        grid_spec=pltpu.PrefetchScalarGridSpec(
            num_scalar_prefetch=1,
            grid=(rows // BS,),
            in_specs=in_specs,
            out_specs=pl.BlockSpec((BS, column_blocks * BS), lambda r, where: (where[0] + r, 0)),
        ),
        out_shape=jax.ShapeDtypeStruct((total_rows, column_blocks * BS), jnp.bfloat16),
        input_output_aliases=aliases,
        compiler_params=pltpu.CompilerParams(vmem_limit_bytes=16 * 1024 * 1024),
        cost_estimate=pl.CostEstimate(
            flops=0, bytes_accessed=rows * (width + column_blocks * BS) * 2, transcendentals=0
        ),
    )(*operands)


def per_device(tokens, norm_gain, kept_blocks, block_cols, row_counts):
    tensor_count = lax.axis_size("tensor")
    devices = lax.axis_size("dp")
    me = lax.axis_index("dp")
    column_blocks = KVH // tensor_count * (GROUP + 2) * HD // BS
    rows_here, slots = block_cols.shape
    shard_rows = rows_here * BS
    seq = tokens.shape[0]
    bits = devices.bit_length() - 1
    y_mask, z_mask = 2, 4
    across = [1 << b for b in range(bits - 1, -1, -1) if (1 << b) not in (y_mask, z_mask)]
    group = devices // 4

    def swap(value, mask):
        return lax.ppermute(value, "dp", [(i, i ^ mask) for i in range(devices)])

    def position(index):
        return index // 8 * 2 + index % 2

    slot_of = jnp.where(
        (block_cols[:, None, :] == jnp.arange(column_blocks)[None, :, None])
        & (jnp.arange(slots)[None, None, :] < row_counts[:, :, None]),
        jnp.arange(slots)[None, None, :] - slots,
        0,
    )
    slot_of = (jnp.sum(slot_of, axis=-1) + slots).astype(jnp.int32)
    slot_all = lax.all_gather(slot_of, "dp", axis=0)

    pieces = {0: kept_blocks}
    for mask in across:
        for known in list(pieces):
            if known == 0:
                pieces[mask] = swap(kept_blocks, mask)
        for known in list(pieces):
            if known not in (0, mask) and known ^ mask not in pieces:
                pieces[known ^ mask] = swap(pieces[known], mask)

    gathered, gain_all = (
        lax.all_gather(tokens, "tensor", axis=1, tiled=True),
        lax.all_gather(norm_gain, "tensor", axis=0, tiled=True),
    )
    floats = gathered.astype(jnp.float32)
    mean_square = jnp.mean(floats * floats, axis=-1, keepdims=True)
    normed = (floats * lax.rsqrt(mean_square + 1e-05) * gain_all.astype(jnp.float32)).astype(
        jnp.bfloat16
    )
    by_owner = normed.reshape(seq, devices // 8, 4, 2, shard_rows)

    def features_of(index):
        part = lax.dynamic_slice_in_dim(by_owner, index % 8 // 2, 1, 2)
        return part.reshape(seq, group * shard_rows)

    d_mask = y_mask | z_mask
    x_far = swap(features_of(me ^ d_mask), d_mask)
    x_y = swap(features_of(me ^ y_mask), y_mask)
    x_z = swap(features_of(me ^ z_mask), z_mask)
    x_own = features_of(me)

    dense = None
    for mask, blocks in pieces.items():
        peer = me ^ mask
        where = jnp.concatenate(
            [
                (position(peer) * rows_here).reshape(1).astype(jnp.int32),
                lax.dynamic_index_in_dim(slot_all, peer, 0, keepdims=False).reshape(-1),
            ]
        )
        dense = place(where, blocks, dense, group * shard_rows, column_blocks)

    def product(left):
        return jnp.dot(left, dense, preferred_element_type=jnp.float32)

    half = column_blocks * BS // 2
    far = product(x_far).astype(jnp.bfloat16)
    via_y = swap(far[:, :half], y_mask)
    via_z = swap(far[:, half:], z_mask)
    part_y = product(x_y)
    y_first = swap(part_y[:, :half].astype(jnp.bfloat16), y_mask)
    part_z = product(x_z)
    z_second = swap(part_z[:, half:].astype(jnp.bfloat16), z_mask)
    y_second = swap(
        (part_y[:, half:] + via_z.astype(jnp.float32)).astype(jnp.bfloat16), y_mask
    )
    z_first = swap(
        (part_z[:, :half] + via_y.astype(jnp.float32)).astype(jnp.bfloat16), z_mask
    )
    own = product(x_own)
    first = own[:, :half] + y_first.astype(jnp.float32) + z_first.astype(jnp.float32)
    second = own[:, half:] + y_second.astype(jnp.float32) + z_second.astype(jnp.float32)
    positions = jnp.arange(seq).astype(jnp.float32)
    return rotate(jnp.concatenate([first, second], axis=1), positions).astype(jnp.bfloat16)


def solution(mesh):
    in_specs = (
        P("dp", "tensor"),
        P("tensor"),
        P("dp", "tensor"),
        P("dp", "tensor"),
        P("dp", "tensor"),
    )
    out_specs = P("dp", "tensor")
    return jax.shard_map(
        per_device, mesh=mesh, in_specs=in_specs, out_specs=out_specs, check_vma=False
    )
```

time: 756 us -> 389 us (0.51)
  waiting for transfers between devices: 477 us -> 48.1 us
  matrix products: 142 us -> 31.2 us
  blocking collectives: 47.7 us -> 153 us
  starting transfers between devices: 0.04 us -> 31.2 us
  Pallas kernels: 0 us -> 14.3 us
  other arithmetic: 14.1 us -> 28.4 us
  local copies, waits for them, and re-layouts: 55.6 us -> 68.6 us
    all_gather x1 -> x0, waiting for transfers between devices: 476 us -> none  [per_device(): block_piece = lax.all_gather(stacked, 'dp', axis=0, tiled=True)]
    dot_general x16 -> x4, matrix products: 142 us -> 31.2 us  [product(): return jnp.dot(left, dense, preferred_element_type=jnp.float32)]
    all_gather x1, blocking collectives: 45.7 us -> 151 us  [per_device(): slot_all = lax.all_gather(slot_of, 'dp', axis=0)]
    ppermute x0 -> x12, waiting for transfers between devices: none -> 47.4 us  [swap(): return lax.ppermute(value, 'dp', [(i, i ^ mask) for i in range(devices)])]
    unnamed x16 -> x27, local copies, waits for them, and re-layouts: 0.41 us -> 36 us
    ppermute x0 -> x12, starting transfers between devices: none -> 31.2 us  [swap(): return lax.ppermute(value, 'dp', [(i, i ^ mask) for i in range(devices)])]
    dynamic_slice x16 -> x2, local copies, waits for them, and re-layouts: 31.1 us -> 5.79 us  [the longest x1 5.78 us: features_of(): part = lax.dynamic_slice_in_dim(by_owner, index % 8 // 2, 1, 2)]
    while x9 -> x0, local copies, waits for them, and re-layouts: 21.3 us -> none
  transfers between devices with their start and end apart: 2 -> 13, of which waited for: 1 -> 4; matrix products, arithmetic and copies ran while one was open for 1% -> 19% of each run, Pallas kernels for 0% -> 4%
where the time goes in v1:
time: 389 us; the launch traced here: 388 us
  blocking collectives  153 us (39%)
  local copies, waits for them, and re-layouts  68.6 us (18%)
  waiting for transfers between devices  48.1 us (12%)
  starting transfers between devices  31.2 us (8%)
  matrix products  31.2 us (8%)
  other arithmetic  28.4 us (7%)
  Pallas kernels  14.3 us (4%)
  between operations  13.6 us (3%)
    all_gather x1, blocking collectives, per_device(): slot_all = lax.all_gather(slot_of, 'dp', axis=0)  151 us
    ppermute x12, waiting for transfers between devices, swap(): return lax.ppermute(value, 'dp', [(i, i ^ mask) for i in range(devices)])  47.4 us
    unnamed x27, local copies, waits for them, and re-layouts  36 us
    ppermute x12, starting transfers between devices, swap(): return lax.ppermute(value, 'dp', [(i, i ^ mask) for i in range(devices)])  31.2 us
    dot_general x4, matrix products, product(): return jnp.dot(left, dense, preferred_element_type=jnp.float32)  31.2 us
    pallas_call x4, Pallas kernels, place(): pl.pallas_call(functools.partial(place_body, slots=slots, column_blocks=c...  14.3 us
    reshape x1, local copies, waits for them, and re-layouts, per_device(): by_owner = normed.reshape(seq, devices // 8, 4, 2, shard_rows)  7.79 us
  transfers between devices with their start and end apart: 13, of which 4 were waited for; matrix products, arithmetic and copies ran while one was open for 19% of the time, Pallas kernels for 4%

profile of v1, /device:TPU:0, one launch (start us, length us, event | category | flops | bytes accessed | tf_op | source)
XLA Modules:
  0.0 388.1 jit_solution(9837600190131539889)
XLA Ops:
  6.5 0.7 all-gather.4.cloned.1.call-update
  7.3 4.1 %collective-permute-start = (bf16[512,3072]{1,0:T(8,128)(2,1)}, bf16[512,3072]{1,0:T(8,128)(2,1)}, u32[]{:S(2)}, u32[]{:S(2)}) collective-permute-start(bf16[512,3072]{1,0:T(8,128)(2,1)} %blocks_ref.1), channel_id=1, source_target_pairs={{0,16},{2,18},{4,20},{6,22},{8,24},{10,26},{12,28},{14,30},{16,0},... | collective-permute-start | bytes 9437192 | tf_op jit(solution)/shard_map/ppermute | solution.py:89
  11.4 1.5 collective-permute-start.2
  12.9 0.7 iota_compare_fusion.1
  13.6 0.8 select_reduce_fusion
  14.4 150.7 %all-gather.1 = s32[16,4,40]{2,1,0:T(4,128)S(1)} all-gather(s32[1,4,40]{2,1,0:T(4,128)S(1)} %add_bitcast_fusion), channel_id=2, replica_groups=mesh['dp'=16,'tensor'=2] {'dp'}, dimensions={0}, use_global_device_ids=true | all-gather | bytes 10880 | tf_op jit(solution)/shard_map/all_gather | solution.py:101
  165.0 0.1 reshape.131
  165.1 2.0 all_gather.11
  167.2 0.1 pad_add_fusion.3.where_ref
  167.3 2.2 collective-permute-start.1
  169.5 3.3 fusion
  172.7 0.2 copy-done.7
  172.9 3.2 fusion.2
  176.1 7.8 %reshape.122 = bf16[256,2,4,2,512]{4,3,2,1,0:T(2,128)(2,1)} reshape(bf16[256,8192]{1,0:T(8,128)(2,1)} %fusion.2) | data formatting | bytes 8388608 | tf_op jit(solution)/shard_map/reshape | solution.py:121
  183.9 5.8 %constant_dynamic-slice_fusion = (bf16[256,2,1,2,512]{4,3,2,1,0:T(2,128)(2,1)}, bf16[256,2,1,2,512]{4,3,2,1,0:T(2,128)(2,1)}, bf16[256,2,1,2,512]{4,3,2,1,0:T(2,128)(2,1)}, bf16[256,2,1,2,512]{4,3,2,1,0:T(2,128)(2,1)}) fusion(bf16[256,2,4,2,512]{4,3,2,1,0:T(2,128)(2,1)} %reshape.122, s32[]{:T(128)S(6)} %select_n.129, s32[]{:T(128)S(6)} %select_n.126, ...), kind=kLoop, calls=%fused_computation.34 | loop fusion | bytes 8388624 | tf_op jit(solution)/shard_map/dynamic_slice | solution.py:124
  189.7 2.6 reshape.134
  192.3 8.0 %collective-permute-start.6 = (bf16[256,2048]{1,0:T(8,128)(2,1)}, bf16[256,2048]{1,0:T(8,128)(2,1)}, u32[]{:S(2)}, u32[]{:S(2)}) collective-permute-start(bf16[256,2048]{1,0:T(8,128)(2,1)} %reshape.134), channel_id=1, source_target_pairs={{0,12},{2,14},{4,8},{6,10},{8,4},{10,6},{12,0},{14,2},{16,28},{18,... | collective-permute-start | bytes 3145736 | tf_op jit(solution)/shard_map/ppermute | solution.py:89
  200.3 2.0 shard_map.55.rest_0_
  202.4 7.0 %copy-done = bf16[2048,5120]{1,0:T(8,128)(2,1)} copy-done((bf16[2048,5120]{1,0:T(8,128)(2,1)}, bf16[2048,5120]{1,0:T(8,128)(2,1)S(1)}, u32[]{:S(2)}) %copy-start) | copy-done | bytes 20971544
  209.4 0.1 reshape.129
  209.5 0.1 reshape.127
  209.5 0.1 reshape.125
  209.6 0.1 pad_add_fusion.2.where_ref
  209.7 0.1 pad_add_fusion.1.where_ref
  209.8 0.1 pad_add_fusion.where_ref
  209.9 0.5 multiply_cosine_fusion
  210.4 0.9 pad_maximum_fusion.1
  211.3 0.1 broadcast_bitcast_fusion
  211.3 7.0 %copy-done.1 = bf16[2048,5120]{1,0:T(8,128)(2,1)S(1)} copy-done((bf16[2048,5120]{1,0:T(8,128)(2,1)S(1)}, bf16[2048,5120]{1,0:T(8,128)(2,1)}, u32[]{:S(2)}) %copy-start.1) | copy-done | bytes 20971544
  218.3 4.0 %shard_map.56.rest_0_ = bf16[2048,5120]{1,0:T(8,128)(2,1)S(1)} custom-call(s32[161]{0:T(256)S(1)} %pad_add_fusion.2.where_ref, bf16[512,3072]{1,0:T(8,128)(2,1)} %collective-permute-done.blocks_ref, bf16[2048,5120]{1,0:T(8,128)(2,1)S(1)} %copy-done.1), custom_call_target="tpu_custom_call", output_to_operand_aliasing={{}: (2, {})} | custom-call | bytes 8388608 | tf_op jit(solution)/shard_map/pallas_call | solution.py:58
  222.3 4.3 %shard_map.57.rest_0_ = bf16[2048,5120]{1,0:T(8,128)(2,1)S(1)} custom-call(s32[161]{0:T(256)S(1)} %pad_add_fusion.1.where_ref, bf16[512,3072]{1,0:T(8,128)(2,1)} %collective-permute-done.2.blocks_ref, bf16[2048,5120]{1,0:T(8,128)(2,1)S(1)} %shard_map.56.rest_0_), custom_call_target="tpu_custom_call", output_to_operand_aliasing={{}: (2, {})} | custom-call | bytes 8388608 | tf_op jit(solution)/shard_map/pallas_call | solution.py:58
  226.6 7.0 %copy-done.2 = bf16[2048,5120]{1,0:T(8,128)(2,1)} copy-done((bf16[2048,5120]{1,0:T(8,128)(2,1)}, bf16[2048,5120]{1,0:T(8,128)(2,1)S(1)}, u32[]{:S(2)}) %copy-start.2) | copy-done | bytes 20971544
  233.6 1.6 reshape.132
  235.3 1.6 reshape.133
  236.9 0.6 collective-permute-start.5
  237.5 0.8 reshape.123
  238.3 7.0 %copy-done.3 = bf16[2048,5120]{1,0:T(8,128)(2,1)S(1)} copy-done((bf16[2048,5120]{1,0:T(8,128)(2,1)S(1)}, bf16[2048,5120]{1,0:T(8,128)(2,1)}, u32[]{:S(2)}) %copy-start.3) | copy-done | bytes 20971544
  245.3 4.0 %shard_map.58 = bf16[2048,5120]{1,0:T(8,128)(2,1)S(1)} custom-call(s32[161]{0:T(256)S(1)} %pad_add_fusion.where_ref, bf16[512,3072]{1,0:T(8,128)(2,1)} %collective-permute-done.1.blocks_ref, bf16[2048,5120]{1,0:T(8,128)(2,1)S(1)} %copy-done.3), custom_call_target="tpu_custom_call", output_to_operand_aliasing={{}: (2, {})} | custom-call | bytes 8388608 | tf_op jit(solution)/shard_map/pallas_call | solution.py:58
  249.3 7.0 %copy-done.4 = bf16[2048,5120]{1,0:T(8,128)(2,1)} copy-done((bf16[2048,5120]{1,0:T(8,128)(2,1)}, bf16[2048,5120]{1,0:T(8,128)(2,1)S(1)}, u32[]{:S(2)}) %copy-start.4) | copy-done | bytes 20971544
  256.3 10.5 %convolution_convert_fusion = bf16[256,5120]{1,0:T(8,128)(2,1)S(1)} fusion(bf16[256,2048]{1,0:T(8,128)(2,1)} %collective-permute-done.6, bf16[2048,5120]{1,0:T(8,128)(2,1)} %copy-done.4), kind=kOutput, calls=%fused_computation.5 | convolution fusion | flops 5370019840 | bytes 24641536 | tf_op jit(solution)/shard_map/dot_general | solution.py:145
  266.8 1.7 fusion.14
  268.5 6.1 %collective-permute-start.9 = (bf16[256,2560]{1,0:T(8,128)(2,1)}, bf16[256,2560]{1,0:T(8,128)(2,1)}, u32[]{:S(2)}, u32[]{:S(2)}) collective-permute-start(bf16[256,2560]{1,0:T(8,128)(2,1)} %get-tuple-element.14), channel_id=1, source_target_pairs={{0,8},{2,10},{4,12},{6,14},{8,0},{10,2},{12,4},{14,6},{16,24},{18,... | collective-permute-start | bytes 3932168 | tf_op jit(solution)/shard_map/ppermute | solution.py:89
  274.6 2.3 collective-permute-start.7
  277.0 6.8 %fusion.17 = f32[256,5120]{1,0:T(8,128)S(1)} fusion(bf16[256,2048]{1,0:T(8,128)(2,1)} %collective-permute-done.5, bf16[2048,5120]{1,0:T(8,128)(2,1)S(1)} %copy-done.5), kind=kOutput, calls=%fused_computation.56 | convolution fusion | flops 5368709120 | bytes 27262976 | tf_op jit(solution)/shard_map/dot_general | solution.py:145
  283.8 1.2 slice.68
  285.0 8.4 %fusion.16 = f32[256,5120]{1,0:T(8,128)} fusion(bf16[256,2048]{1,0:T(8,128)(2,1)} %collective-permute-done.3, bf16[2048,5120]{1,0:T(8,128)(2,1)S(1)} %copy-done.5), kind=kOutput, calls=%fused_computation.55 | convolution fusion | flops 5368709120 | bytes 27262976 | tf_op jit(solution)/shard_map/dot_general | solution.py:145
  293.3 3.0 slice.69
  296.3 2.0 collective-permute-start.4
  298.3 6.3 %collective-permute-done.9 = bf16[256,2560]{1,0:T(8,128)(2,1)} collective-permute-done((bf16[256,2560]{1,0:T(8,128)(2,1)}, bf16[256,2560]{1,0:T(8,128)(2,1)}, u32[]{:S(2)}, u32[]{:S(2)}) %collective-permute-start.9) | collective-permute-done | bytes 1310752 | tf_op jit(solution)/shard_map/ppermute | solution.py:89
  304.6 3.5 fusion.6
  308.0 2.3 collective-permute-start.10
  310.4 2.7 fusion.8
  313.0 2.1 collective-permute-start.8
  315.1 5.6 %fusion.15 = f32[256,5120]{1,0:T(8,128)S(1)} fusion(bf16[256,2048]{1,0:T(8,128)(2,1)S(1)} %reshape.123, bf16[2048,5120]{1,0:T(8,128)(2,1)S(1)} %copy-done.5), kind=kOutput, calls=%fused_computation.54 | convolution fusion | flops 5368709120 | bytes 27262976 | tf_op jit(solution)/shard_map/dot_general | solution.py:145
  320.7 12.0 %collective-permute-done.11 = bf16[256,2560]{1,0:T(8,128)(2,1)} collective-permute-done((bf16[256,2560]{1,0:T(8,128)(2,1)}, bf16[256,2560]{1,0:T(8,128)(2,1)}, u32[]{:S(2)}, u32[]{:S(2)}) %collective-permute-start.11) | collective-permute-done | bytes 1310752 | tf_op jit(solution)/shard_map/ppermute | solution.py:89
  332.7 2.4 collective-permute-done.4
  335.0 26.7 %collective-permute-done.10 = bf16[256,2560]{1,0:T(8,128)(2,1)} collective-permute-done((bf16[256,2560]{1,0:T(8,128)(2,1)}, bf16[256,2560]{1,0:T(8,128)(2,1)}, u32[]{:S(2)}, u32[]{:S(2)}) %collective-permute-start.10) | collective-permute-done | bytes 1310752 | tf_op jit(solution)/shard_map/ppermute | solution.py:89
  361.7 3.6 fusion.9
  365.4 0.4 fusion.5
  365.8 0.9 copy.10
  366.8 5.7 %fusion.13 = (f32[256,40,64]{2,1,0:T(8,128)}, f32[256,40,64]{2,1,0:T(8,128)}) fusion(f32[256,40,128]{2,1,0:T(8,128)S(1)} %bitcast.32), kind=kLoop, calls=%fused_computation.52 | loop fusion | bytes 10485760 | tf_op jit(solution)/shard_map/jit(_roll_static)/slice | solution.py:30
  372.4 5.5 %maximum_multiply_fusion = f32[256,40,128]{2,1,0:T(8,128)S(1)} fusion(f32[256,40,64]{2,1,0:T(8,128)} %get-tuple-element.6, f32[256,40,64]{2,1,0:T(8,128)} %get-tuple-element.5, f32[256,128]{1,0:T(8,128)S(1)} %copy-done.11), kind=kLoop, calls=%fused_computation.11 | loop fusion | flops 2621440 | bytes 10616832 | tf_op jit(solution)/shard_map/mul | solution.py:31
  377.9 0.3 mul.116
  378.3 3.0 fusion.4
  (40 shorter events, 0.1 us)
Async XLA Ops:
  6.5 162.9 %all-gather.4.cloned.1.call-start = ((), (), s32[]{:S(2)}) async-start(), calls=%async_computation | async-start | bytes 6291456 | tf_op jit(solution)/shard_map/all_gather | solution.py:113
  7.3 160.0 %collective-permute-start = (bf16[512,3072]{1,0:T(8,128)(2,1)}, bf16[512,3072]{1,0:T(8,128)(2,1)}, u32[]{:S(2)}, u32[]{:S(2)}) collective-permute-start(bf16[512,3072]{1,0:T(8,128)(2,1)} %blocks_ref.1), channel_id=1, source_target_pairs={{0,16},{2,18},{4,20},{6,22},{8,24},{10,26},{12,28},{14,30},{16,0},... | collective-permute-start | bytes 9437192 | tf_op jit(solution)/shard_map/ppermute | solution.py:89
  11.4 211.0 %collective-permute-start.2 = (bf16[512,3072]{1,0:T(8,128)(2,1)}, bf16[512,3072]{1,0:T(8,128)(2,1)}, u32[]{:S(2)}, u32[]{:S(2)}) collective-permute-start(bf16[512,3072]{1,0:T(8,128)(2,1)} %blocks_ref.1), channel_id=1, source_target_pairs={{0,2},{2,0},{4,6},{6,4},{8,10},{10,8},{12,14},{14,12},{16,18},{18,... | collective-permute-start | bytes 9437192 | tf_op jit(solution)/shard_map/ppermute | solution.py:89
  167.3 71.1 %collective-permute-start.1 = (bf16[512,3072]{1,0:T(8,128)(2,1)}, bf16[512,3072]{1,0:T(8,128)(2,1)}, u32[]{:S(2)}, u32[]{:S(2)}) collective-permute-start(bf16[512,3072]{1,0:T(8,128)(2,1)} %collective-permute-done.blocks_ref), channel_id=1, source_target_pairs={{0,2},{2,0},{4,6},{6,4},{8,10},{10,8},{12,14},{14,12},{16,18},{18,... | collective-permute-start | bytes 9437192 | tf_op jit(solution)/shard_map/ppermute | solution.py:89
  169.5 3.4 copy-start.7
  183.9 16.4 %copy-start.6 = (bf16[512,3072]{1,0:T(8,128)(2,1)S(1)}, bf16[512,3072]{1,0:T(8,128)(2,1)}, u32[]{:S(2)}) copy-start(bf16[512,3072]{1,0:T(8,128)(2,1)} %blocks_ref.1) | copy-start | bytes 9437188
  192.3 64.0 %collective-permute-start.6 = (bf16[256,2048]{1,0:T(8,128)(2,1)}, bf16[256,2048]{1,0:T(8,128)(2,1)}, u32[]{:S(2)}, u32[]{:S(2)}) collective-permute-start(bf16[256,2048]{1,0:T(8,128)(2,1)} %reshape.134), channel_id=1, source_target_pairs={{0,12},{2,14},{4,8},{6,10},{8,4},{10,6},{12,0},{14,2},{16,28},{18,... | collective-permute-start | bytes 3145736 | tf_op jit(solution)/shard_map/ppermute | solution.py:89
  202.4 7.0 %copy-start = (bf16[2048,5120]{1,0:T(8,128)(2,1)}, bf16[2048,5120]{1,0:T(8,128)(2,1)S(1)}, u32[]{:S(2)}) copy-start(bf16[2048,5120]{1,0:T(8,128)(2,1)S(1)} %shard_map.55.rest_0_) | copy-start | bytes 62914564
  211.3 7.0 %copy-start.1 = (bf16[2048,5120]{1,0:T(8,128)(2,1)S(1)}, bf16[2048,5120]{1,0:T(8,128)(2,1)}, u32[]{:S(2)}) copy-start(bf16[2048,5120]{1,0:T(8,128)(2,1)} %copy-done) | copy-start | bytes 62914564
  222.3 11.3 %copy-start.10 = (bf16[256,2,1,2,512]{4,3,2,1,0:T(2,128)(2,1)S(1)}, bf16[256,2,1,2,512]{4,3,2,1,0:T(2,128)(2,1)}, u32[]{:S(2)}) copy-start(bf16[256,2,1,2,512]{4,3,2,1,0:T(2,128)(2,1)} %get-tuple-element.11) | copy-start | bytes 3145732
  222.3 13.0 %copy-start.9 = (bf16[256,2,1,2,512]{4,3,2,1,0:T(2,128)(2,1)S(1)}, bf16[256,2,1,2,512]{4,3,2,1,0:T(2,128)(2,1)}, u32[]{:S(2)}) copy-start(bf16[256,2,1,2,512]{4,3,2,1,0:T(2,128)(2,1)} %get-tuple-element.10) | copy-start | bytes 3145732
  222.3 15.2 %copy-start.8 = (bf16[256,2,1,2,512]{4,3,2,1,0:T(2,128)(2,1)S(1)}, bf16[256,2,1,2,512]{4,3,2,1,0:T(2,128)(2,1)}, u32[]{:S(2)}) copy-start(bf16[256,2,1,2,512]{4,3,2,1,0:T(2,128)(2,1)} %get-tuple-element.12) | copy-start | bytes 3145732
  226.6 7.0 %copy-start.2 = (bf16[2048,5120]{1,0:T(8,128)(2,1)}, bf16[2048,5120]{1,0:T(8,128)(2,1)S(1)}, u32[]{:S(2)}) copy-start(bf16[2048,5120]{1,0:T(8,128)(2,1)S(1)} %shard_map.57.rest_0_) | copy-start | bytes 62914564
  235.3 49.7 %collective-permute-start.3 = (bf16[256,2048]{1,0:T(8,128)(2,1)}, bf16[256,2048]{1,0:T(8,128)(2,1)}, u32[]{:S(2)}, u32[]{:S(2)}) collective-permute-start(bf16[256,2048]{1,0:T(8,128)(2,1)} %reshape.132), channel_id=1, source_target_pairs={{0,4},{2,6},{4,0},{6,2},{8,12},{10,14},{12,8},{14,10},{16,20},{18,... | collective-permute-start | bytes 3145736 | tf_op jit(solution)/shard_map/ppermute | solution.py:89
  236.9 40.1 %collective-permute-start.5 = (bf16[256,2048]{1,0:T(8,128)(2,1)}, bf16[256,2048]{1,0:T(8,128)(2,1)}, u32[]{:S(2)}, u32[]{:S(2)}) collective-permute-start(bf16[256,2048]{1,0:T(8,128)(2,1)} %reshape.133), channel_id=1, source_target_pairs={{0,8},{2,10},{4,12},{6,14},{8,0},{10,2},{12,4},{14,6},{16,24},{18,... | collective-permute-start | bytes 3145736 | tf_op jit(solution)/shard_map/ppermute | solution.py:89
  238.3 7.0 %copy-start.3 = (bf16[2048,5120]{1,0:T(8,128)(2,1)S(1)}, bf16[2048,5120]{1,0:T(8,128)(2,1)}, u32[]{:S(2)}) copy-start(bf16[2048,5120]{1,0:T(8,128)(2,1)} %copy-done.2) | copy-start | bytes 62914564
  249.3 7.0 %copy-start.4 = (bf16[2048,5120]{1,0:T(8,128)(2,1)}, bf16[2048,5120]{1,0:T(8,128)(2,1)S(1)}, u32[]{:S(2)}) copy-start(bf16[2048,5120]{1,0:T(8,128)(2,1)S(1)} %shard_map.58) | copy-start | bytes 62914564
  256.3 20.7 %copy-start.5 = (bf16[2048,5120]{1,0:T(8,128)(2,1)S(1)}, bf16[2048,5120]{1,0:T(8,128)(2,1)}, u32[]{:S(2)}) copy-start(bf16[2048,5120]{1,0:T(8,128)(2,1)} %copy-done.4) | copy-start | bytes 62914564
  268.5 36.1 %collective-permute-start.9 = (bf16[256,2560]{1,0:T(8,128)(2,1)}, bf16[256,2560]{1,0:T(8,128)(2,1)}, u32[]{:S(2)}, u32[]{:S(2)}) collective-permute-start(bf16[256,2560]{1,0:T(8,128)(2,1)} %get-tuple-element.14), channel_id=1, source_target_pairs={{0,8},{2,10},{4,12},{6,14},{8,0},{10,2},{12,4},{14,6},{16,24},{18,... | collective-permute-start | bytes 3932168 | tf_op jit(solution)/shard_map/ppermute | solution.py:89
  274.6 35.7 %collective-permute-start.7 = (bf16[256,2560]{1,0:T(8,128)(2,1)}, bf16[256,2560]{1,0:T(8,128)(2,1)}, u32[]{:S(2)}, u32[]{:S(2)}) collective-permute-start(bf16[256,2560]{1,0:T(8,128)(2,1)} %get-tuple-element.13), channel_id=1, source_target_pairs={{0,4},{2,6},{4,0},{6,2},{8,12},{10,14},{12,8},{14,10},{16,20},{18,... | collective-permute-start | bytes 3932168 | tf_op jit(solution)/shard_map/ppermute | solution.py:89
  285.0 47.7 %collective-permute-start.11 = (bf16[256,2560]{1,0:T(8,128)(2,1)}, bf16[256,2560]{1,0:T(8,128)(2,1)}, u32[]{:S(2)}, u32[]{:S(2)}) collective-permute-start(bf16[256,2560]{1,0:T(8,128)(2,1)} %slice.68), channel_id=1, source_target_pairs={{0,8},{2,10},{4,12},{6,14},{8,0},{10,2},{12,4},{14,6},{16,24},{18,... | collective-permute-start | bytes 3932168 | tf_op jit(solution)/shard_map/ppermute | solution.py:89
  296.3 38.7 %collective-permute-start.4 = (bf16[256,2560]{1,0:T(8,128)(2,1)}, bf16[256,2560]{1,0:T(8,128)(2,1)}, u32[]{:S(2)}, u32[]{:S(2)}) collective-permute-start(bf16[256,2560]{1,0:T(8,128)(2,1)} %slice.69), channel_id=1, source_target_pairs={{0,4},{2,6},{4,0},{6,2},{8,12},{10,14},{12,8},{14,10},{16,20},{18,... | collective-permute-start | bytes 3932168 | tf_op jit(solution)/shard_map/ppermute | solution.py:89
  308.0 53.7 %collective-permute-start.10 = (bf16[256,2560]{1,0:T(8,128)(2,1)}, bf16[256,2560]{1,0:T(8,128)(2,1)}, u32[]{:S(2)}, u32[]{:S(2)}) collective-permute-start(bf16[256,2560]{1,0:T(8,128)(2,1)} %fusion.6), channel_id=1, source_target_pairs={{0,4},{2,6},{4,0},{6,2},{8,12},{10,14},{12,8},{14,10},{16,20},{18,... | collective-permute-start | bytes 3932168 | tf_op jit(solution)/shard_map/ppermute | solution.py:89
  313.0 48.7 %collective-permute-start.8 = (bf16[256,2560]{1,0:T(8,128)(2,1)}, bf16[256,2560]{1,0:T(8,128)(2,1)}, u32[]{:S(2)}, u32[]{:S(2)}) collective-permute-start(bf16[256,2560]{1,0:T(8,128)(2,1)} %fusion.8), channel_id=1, source_target_pairs={{0,8},{2,10},{4,12},{6,14},{8,0},{10,2},{12,4},{14,6},{16,24},{18,... | collective-permute-start | bytes 3932168 | tf_op jit(solution)/shard_map/ppermute | solution.py:89
  366.7 5.7 %copy-start.11 = (f32[256,128]{1,0:T(8,128)S(1)}, f32[256,128]{1,0:T(8,128)}, u32[]{:S(2)}) copy-start(f32[256,128]{1,0:T(8,128)} %get-tuple-element.23) | copy-start | bytes 393220
  372.4 5.5 %copy-start.12 = (f32[256,128]{1,0:T(8,128)S(1)}, f32[256,128]{1,0:T(8,128)}, u32[]{:S(2)}) copy-start(f32[256,128]{1,0:T(8,128)} %get-tuple-element.22) | copy-start | bytes 393220
Sparse Core Ops, SparseCore 0:
  8.9 16.3 all-gather.3

commit v2 on v1

v2 whole, which is shorter than its diff:
```python
import functools

import jax
import jax.numpy as jnp
from jax import lax
from jax.experimental import pallas as pl
from jax.experimental.pallas import tpu as pltpu
from jax.sharding import PartitionSpec as P

KVH = 8
GROUP = 8
HD = 128
BS = 128


rope_theta = 500000.0


def place_body(where_ref, blocks_ref, *rest, slots, column_blocks):
    out_ref = rest[-1]
    row = pl.program_id(0)
    for column in range(column_blocks):
        slot = where_ref[1 + row * column_blocks + column]
        start = pl.multiple_of(jnp.minimum(slot, slots - 1) * BS, BS)
        block = blocks_ref[:, pl.ds(start, BS)]
        out_ref[:, column * BS : (column + 1) * BS] = jnp.where(
            slot < slots, block, jnp.zeros_like(block)
        )


def place(where, blocks, dense, total_rows, column_blocks):
    rows, width = blocks.shape
    slots = width // BS
    in_specs = [pl.BlockSpec((BS, width), lambda r, where: (r, 0))]
    operands = [where, blocks]
    aliases = {}
    if dense is not None:
        in_specs.append(pl.BlockSpec(memory_space=pl.ANY))
        operands.append(dense)
        aliases = {2: 0}
    return pl.pallas_call(
        functools.partial(place_body, slots=slots, column_blocks=column_blocks),
        grid_spec=pltpu.PrefetchScalarGridSpec(
            num_scalar_prefetch=1,
            grid=(rows // BS,),
            in_specs=in_specs,
            out_specs=pl.BlockSpec((BS, column_blocks * BS), lambda r, where: (where[0] + r, 0)),
        ),
        out_shape=jax.ShapeDtypeStruct((total_rows, column_blocks * BS), jnp.bfloat16),
        input_output_aliases=aliases,
        compiler_params=pltpu.CompilerParams(vmem_limit_bytes=56 * 1024 * 1024),
        cost_estimate=pl.CostEstimate(
            flops=0, bytes_accessed=rows * (width + column_blocks * BS) * 2, transcendentals=0
        ),
    )(*operands)


def finish_body(own, a_first, a_second, z_first, z_second, cosine, sine, out_ref, *, steps, heads):
    step = pl.program_id(0)
    cos_here = cosine[...]
    sin_here = sine[...]

    def write(from_a, from_z):
        for head in range(heads):
            lanes = slice(head * HD, (head + 1) * HD)
            mixed = (
                own[:, lanes]
                + from_a[:, lanes].astype(jnp.float32)
                + from_z[:, lanes].astype(jnp.float32)
            )
            turned = mixed * cos_here + pltpu.roll(mixed, HD // 2, 1) * sin_here
            rotated = (step * heads + head) % (GROUP + 2) < GROUP + 1
            out_ref[:, lanes] = jnp.where(rotated, turned, mixed).astype(jnp.bfloat16)

    @pl.when(step < steps // 2)
    def _():
        write(a_first, z_first)

    @pl.when(step >= steps // 2)
    def _():
        write(a_second, z_second)


def finish(own, a_first, a_second, z_first, z_second):
    rows, width = own.shape
    heads = (GROUP + 2) // 2
    block = heads * HD
    steps = width // block
    half_steps = steps // 2
    half_size = HD // 2
    inverse_freq = rope_theta ** (-(jnp.arange(half_size).astype(jnp.float32) * 2.0 / HD))
    angles = jnp.arange(rows).astype(jnp.float32)[:, None] * inverse_freq[None, :]
    cosine = jnp.cos(angles)
    sine = jnp.sin(angles)
    cos_full = jnp.concatenate([cosine, cosine], axis=-1)
    sin_full = jnp.concatenate([-sine, sine], axis=-1)
    low = pl.BlockSpec((rows, block), lambda j: (0, jnp.minimum(j, half_steps - 1)))
    high = pl.BlockSpec((rows, block), lambda j: (0, jnp.maximum(j - half_steps, 0)))
    table = pl.BlockSpec((rows, HD), lambda j: (0, 0))
    return pl.pallas_call(
        functools.partial(finish_body, steps=steps, heads=heads),
        grid=(steps,),
        in_specs=[pl.BlockSpec((rows, block), lambda j: (0, j)), low, high, low, high, table, table],
        out_specs=pl.BlockSpec((rows, block), lambda j: (0, j)),
        out_shape=jax.ShapeDtypeStruct((rows, width), jnp.bfloat16),
        compiler_params=pltpu.CompilerParams(vmem_limit_bytes=48 * 1024 * 1024),
        cost_estimate=pl.CostEstimate(
            flops=rows * width * 6, bytes_accessed=rows * width * 10, transcendentals=0
        ),
    )(own, a_first, a_second, z_first, z_second, cos_full, sin_full)


def per_device(tokens, norm_gain, kept_blocks, block_cols, row_counts):
    tensor_count = lax.axis_size("tensor")
    devices = lax.axis_size("dp")
    me = lax.axis_index("dp")
    column_blocks = KVH // tensor_count * (GROUP + 2) * HD // BS
    rows_here, slots = block_cols.shape
    shard_rows = rows_here * BS
    group = devices // 4
    odd = lax.axis_index("tensor") % 2
    z_bit = (4, 4)
    sum_bit = (2, 1)
    weight_bit = (1, 2)
    far_bits = (6, 5)
    across = [(1 << b, 1 << b) for b in range(devices.bit_length() - 2, 2, -1)]

    def swap(value, masks):
        pairs = [
            (i * tensor_count + t, (i ^ masks[t % 2]) * tensor_count + t)
            for i in range(devices)
            for t in range(tensor_count)
        ]
        return lax.ppermute(value, ("dp", "tensor"), pairs)

    def mine(masks):
        return jnp.where(odd == 1, masks[1], masks[0])

    def position(index):
        return index // 8 * 2 + jnp.where(index & mine(weight_bit) > 0, 1, 0)

    offsets = [(0, 0)]
    for masks in across:
        offsets += [(e ^ masks[0], o ^ masks[1]) for e, o in offsets]
    offsets += [(e ^ weight_bit[0], o ^ weight_bit[1]) for e, o in offsets]

    slot_of = jnp.where(
        (block_cols[:, None, :] == jnp.arange(column_blocks)[None, :, None])
        & (jnp.arange(slots)[None, None, :] < row_counts[:, :, None]),
        jnp.arange(slots)[None, None, :] - slots,
        0,
    )
    slot_of = (jnp.sum(slot_of, axis=-1) + slots).astype(jnp.int32)
    slots_from = [slot_of] + [swap(slot_of, masks) for masks in offsets[1:]]
    tied = lax.optimization_barrier([kept_blocks] + slots_from)
    kept_blocks, slots_from = tied[0], tied[1:]

    order = []
    for row in range(rows_here):
        chunk = kept_blocks[row * BS : (row + 1) * BS]
        held = {(0, 0): chunk}
        for masks in across:
            for known in list(held):
                held[(known[0] ^ masks[0], known[1] ^ masks[1])] = swap(held[known], masks)
        for known in list(held):
            held[(known[0] ^ weight_bit[0], known[1] ^ weight_bit[1])] = swap(
                held[known], weight_bit
            )
        order += [(row, masks, held[masks]) for masks in offsets]

    gathered, gain_all = (
        lax.all_gather(tokens, "tensor", axis=1, tiled=True),
        lax.all_gather(norm_gain, "tensor", axis=0, tiled=True),
    )
    floats = gathered.astype(jnp.float32)
    mean_square = jnp.mean(floats * floats, axis=-1, keepdims=True)
    normed = (floats * lax.rsqrt(mean_square + 1e-05) * gain_all.astype(jnp.float32)).astype(
        jnp.bfloat16
    )

    def features_of(index):
        fixed = index & mine(far_bits)
        parts = []
        for place_at in range(group):
            owner = fixed + place_at // 2 * 8 + place_at % 2 * mine(weight_bit)
            parts.append(lax.dynamic_slice_in_dim(normed, owner * shard_rows, shard_rows, 1))
        return jnp.concatenate(parts, axis=1)

    x_far = swap(features_of(me ^ mine(far_bits)), far_bits)
    x_z = swap(features_of(me ^ 4), z_bit)
    x_a = swap(features_of(me ^ mine(sum_bit)), sum_bit)
    x_own = features_of(me)

    dense = None
    slot_table = dict(zip(offsets, slots_from))
    for row, masks, blocks in order:
        peer = me ^ mine(masks)
        where = jnp.concatenate(
            [
                (position(peer) * rows_here + row).reshape(1).astype(jnp.int32),
                slot_table[masks][row],
            ]
        )
        dense = place(where, blocks, dense, group * shard_rows, column_blocks)

    def product(left):
        return jnp.dot(left, dense, preferred_element_type=jnp.float32)

    half = column_blocks * BS // 2
    far = product(x_far).astype(jnp.bfloat16)
    far_first = swap(far[:, :half], sum_bit)
    far_second = swap(far[:, half:], sum_bit)
    part_z = product(x_z)
    part_a = product(x_a).astype(jnp.bfloat16)
    a_first = swap(part_a[:, :half], sum_bit)
    a_second = swap(part_a[:, half:], sum_bit)
    z_first = swap(
        (part_z[:, :half] + far_first.astype(jnp.float32)).astype(jnp.bfloat16), z_bit
    )
    z_second = swap(
        (part_z[:, half:] + far_second.astype(jnp.float32)).astype(jnp.bfloat16), z_bit
    )
    return finish(product(x_own), a_first, a_second, z_first, z_second)


def solution(mesh):
    in_specs = (
        P("dp", "tensor"),
        P("tensor"),
        P("dp", "tensor"),
        P("dp", "tensor"),
        P("dp", "tensor"),
    )
    out_specs = P("dp", "tensor")
    return jax.shard_map(
        per_device, mesh=mesh, in_specs=in_specs, out_specs=out_specs, check_vma=False
    )
```

time: 389 us -> 339 us (0.87)
  blocking collectives: 153 us -> 2.01 us
  waiting for transfers between devices: 48.1 us -> 165 us
  local copies, waits for them, and re-layouts: 68.6 us -> 8.48 us
  Pallas kernels: 14.3 us -> 59.2 us
  matrix products: 31.2 us -> 40.3 us
  other arithmetic: 28.4 us -> 21.9 us
    all_gather x1 -> x0, blocking collectives: 151 us -> none  [per_device(): slot_all = lax.all_gather(slot_of, 'dp', axis=0)]
    ppermute x12 -> x24, waiting for transfers between devices: 47.4 us -> 164 us  [swap(): return lax.ppermute(value, ('dp', 'tensor'), pairs)]
    pallas_call x4 -> x16, Pallas kernels: 14.3 us -> 51.9 us  [place(): pl.pallas_call(functools.partial(place_body, slots=slots, column_blocks=c...]
    unnamed x27 -> x52, local copies, waits for them, and re-layouts: 36 us -> 1.92 us
    reshape x9 -> x0, local copies, waits for them, and re-layouts: 14.8 us -> none  [the longest x1 7.79 us: per_device(): by_owner = normed.reshape(seq, devices // 8, 4, 2, shard_rows)]
    concatenate x5 -> x20, other arithmetic: 1.17 us -> 13.3 us  [the longest x16 9.68 us: per_device(): jnp.concatenate([(position(peer) * rows_here + row).reshape(1).astype(jnp...]
    dot_general x4, matrix products: 31.2 us -> 40.3 us  [product(): return jnp.dot(left, dense, preferred_element_type=jnp.float32)]
    pallas_call x0 -> x1, Pallas kernels: none -> 7.29 us  [finish(): pl.pallas_call(functools.partial(finish_body, steps=steps, heads=heads),...]
  transfers between devices with their start and end apart: 13 -> 25, of which waited for: 4 -> 10; matrix products, arithmetic and copies ran while one was open for 19% -> 20% of each run, Pallas kernels for 4% -> 15%
where the time goes in v2:
time: 339 us; the launch traced here: 338 us
  waiting for transfers between devices  165 us (49%)
  Pallas kernels  59.2 us (17%)
  matrix products  40.3 us (12%)
  starting transfers between devices  27.8 us (8%)
  other arithmetic  21.9 us (6%)
  between operations  13.8 us (4%)
  local copies, waits for them, and re-layouts  8.48 us (3%)
    ppermute x24, waiting for transfers between devices, swap(): return lax.ppermute(value, ('dp', 'tensor'), pairs)  164 us
    pallas_call x16, Pallas kernels, place(): pl.pallas_call(functools.partial(place_body, slots=slots, column_blocks=c...  51.9 us
    dot_general x4, matrix products, product(): return jnp.dot(left, dense, preferred_element_type=jnp.float32)  40.3 us
    ppermute x24, starting transfers between devices, swap(): return lax.ppermute(value, ('dp', 'tensor'), pairs)  27.8 us
    concatenate x16, other arithmetic, per_device(): jnp.concatenate([(position(peer) * rows_here + row).reshape(1).astype(jnp...  9.68 us
    pallas_call x1, Pallas kernels, finish(): pl.pallas_call(functools.partial(finish_body, steps=steps, heads=heads),...  7.29 us
  transfers between devices with their start and end apart: 25, of which 10 were waited for; matrix products, arithmetic and copies ran while one was open for 20% of the time, Pallas kernels for 15%

profile of v2, /device:TPU:0, one launch (start us, length us, event | category | flops | bytes accessed | tf_op | source)
XLA Modules:
  0.0 338.3 jit_solution(8053809177532007772)
XLA Ops:
  6.5 0.7 all-gather.2.cloned.1.call-update
  7.3 0.7 iota_compare_fusion.1
  8.0 0.8 select_reduce_fusion
  8.8 4.1 %collective-permute-start = (s32[4,40]{1,0:T(4,128)S(1)}, s32[4,40]{1,0:T(4,128)S(1)}, u32[]{:S(2)}, u32[]{:S(2)}) collective-permute-start(s32[4,40]{1,0:T(4,128)S(1)} %broadcast_add_fusion), channel_id=1, source_target_pairs={{0,16},{1,17},{2,18},{3,19},{4,20},{5,21},{6,22},{7,23},{8,24},{9,... | collective-permute-start | bytes 1928 | tf_op jit(solution)/shard_map/ppermute | solution.py:134
  12.9 1.5 collective-permute-start.1
  14.4 2.0 all_gather.7
  17.3 2.5 collective-permute-done.2
  19.8 3.4 fusion.16
  23.6 1.5 collective-permute-start.14
  25.0 1.7 collective-permute-start.9
  26.7 1.4 collective-permute-start.11
  28.8 3.2 shard_map.55.rest_0_
  32.3 0.7 pad_add_fusion.14.where_ref
  35.3 0.7 pad_add_fusion.9.where_ref
  38.4 3.3 fusion
  41.6 51.9 %collective-permute-done.12.blocks_ref = bf16[128,3072]{1,0:T(8,128)(2,1)} collective-permute-done((bf16[128,3072]{1,0:T(8,128)(2,1)S(1)}, bf16[128,3072]{1,0:T(8,128)(2,1)}, u32[]{:S(2)}, u32[]{:S(2)}) %collective-permute-start.12) | collective-permute-done | bytes 786464 | tf_op jit(solution)/shard_map/ppermute | solution.py:134
  93.5 1.5 collective-permute-start.13
  95.0 32.2 %collective-permute-done.9.blocks_ref = bf16[128,3072]{1,0:T(8,128)(2,1)} collective-permute-done((bf16[128,3072]{1,0:T(8,128)(2,1)S(1)}, bf16[128,3072]{1,0:T(8,128)(2,1)}, u32[]{:S(2)}, u32[]{:S(2)}) %collective-permute-start.9) | collective-permute-done | bytes 786464 | tf_op jit(solution)/shard_map/ppermute | solution.py:134
  127.2 1.5 collective-permute-start.10
  128.7 1.2 fusion.2
  129.9 1.8 constant_dynamic-slice_fusion.3
  132.3 11.7 %collective-permute-done.6.blocks_ref = bf16[128,3072]{1,0:T(8,128)(2,1)S(1)} collective-permute-done((bf16[128,3072]{1,0:T(8,128)(2,1)S(1)}, bf16[128,3072]{1,0:T(8,128)(2,1)S(1)}, u32[]{:S(2)}, u32[]{:S(2)}) %collective-permute-start.6) | collective-permute-done | bytes 786464 | tf_op jit(solution)/shard_map/ppermute | solution.py:134
  144.0 1.5 collective-permute-start.5
  145.5 14.3 %collective-permute-done.3.blocks_ref = bf16[128,3072]{1,0:T(8,128)(2,1)} collective-permute-done((bf16[128,3072]{1,0:T(8,128)(2,1)}, bf16[128,3072]{1,0:T(8,128)(2,1)}, u32[]{:S(2)}, u32[]{:S(2)}) %collective-permute-start.3) | collective-permute-done | bytes 786464 | tf_op jit(solution)/shard_map/ppermute | solution.py:134
  159.8 1.5 collective-permute-start.7
  161.8 1.1 pad_maximum_fusion.2
  162.9 1.4 collective-permute-start.19
  167.4 3.2 shard_map.56.rest_0_
  170.6 3.2 shard_map.57.rest_0_
  173.9 3.2 shard_map.58.rest_0_
  177.1 3.2 shard_map.59.rest_0_
  180.3 3.3 shard_map.60.rest_0_
  183.6 3.3 shard_map.61.rest_0_
  186.9 3.2 shard_map.62.rest_0_
  190.1 3.2 shard_map.63.rest_0_
  193.3 3.2 shard_map.64.rest_0_
  196.5 0.9 copy-done.15
  197.4 3.3 shard_map.65.rest_0_
  200.7 0.9 copy-done.16
  201.6 3.3 shard_map.66.rest_0_
  204.8 3.2 shard_map.67.rest_0_
  208.1 3.3 shard_map.68.rest_0_
  211.3 3.2 shard_map.69.rest_0_
  214.6 3.4 shard_map.70
  218.0 1.1 pad_maximum_fusion.1
  219.1 1.3 collective-permute-start.18
  220.5 1.2 pad_maximum_fusion
  221.7 0.8 collective-permute-start.15
  222.5 10.9 %convolution_convert_fusion = bf16[256,5120]{1,0:T(8,128)(2,1)S(1)} fusion(bf16[256,2048]{1,0:T(8,128)(2,1)} %collective-permute-done.19, bf16[2048,5120]{1,0:T(8,128)(2,1)} %shard_map.70), kind=kOutput, calls=%fused_computation.5 | convolution fusion | flops 5370019840 | bytes 24641536 | tf_op jit(solution)/shard_map/dot_general | solution.py:207
  233.4 1.2 fusion.17
  234.7 1.3 collective-permute-start.20
  236.0 0.7 collective-permute-start.22
  236.9 6.8 %convolution_convert_fusion.1 = bf16[256,5120]{1,0:T(8,128)(2,1)S(1)} fusion(bf16[256,2048]{1,0:T(8,128)(2,1)} %collective-permute-done.15, bf16[2048,5120]{1,0:T(8,128)(2,1)S(1)} %bitcast.57), kind=kOutput, calls=%fused_computation.6 | convolution fusion | flops 5370019840 | bytes 24641536 | tf_op jit(solution)/shard_map/dot_general | solution.py:207
  244.0 1.2 collective-permute-start.16
  245.2 0.9 collective-permute-start.17
  246.1 10.1 %fusion.19 = f32[256,5120]{1,0:T(8,128)S(1)} fusion(bf16[256,2048]{1,0:T(8,128)(2,1)} %collective-permute-done.18, bf16[2048,5120]{1,0:T(8,128)(2,1)} %shard_map.70), kind=kOutput, calls=%fused_computation.88 | convolution fusion | flops 5368709120 | bytes 27262976 | tf_op jit(solution)/shard_map/dot_general | solution.py:207
  256.3 10.4 %collective-permute-done.22 = bf16[256,2560]{1,0:T(8,128)(2,1)} collective-permute-done((bf16[256,2560]{1,0:T(8,128)(2,1)S(1)}, bf16[256,2560]{1,0:T(8,128)(2,1)}, u32[]{:S(2)}, u32[]{:S(2)}) %collective-permute-start.22) | collective-permute-done | bytes 1310752 | tf_op jit(solution)/shard_map/ppermute | solution.py:134
  266.6 2.1 fusion.3
  269.1 1.7 collective-permute-start.23
  270.8 12.4 %fusion.5.own = f32[256,5120]{1,0:T(8,128)} fusion(bf16[2048,5120]{1,0:T(8,128)(2,1)} %shard_map.70, bf16[256,512]{1,0:T(8,128)(2,1)S(1)} %copy-done.17, bf16[256,512]{1,0:T(8,128)(2,1)S(1)} %copy-done.18, bf16[256,512]{1,0:T(8,128)(2,1)S(1)} %copy-done.19, bf16[256,512]{1,0:T(8,128)(2,1)S(1)} %copy-done.20), kind=kOutput, calls=%fused_computation.11 | convolution fusion | flops 5372903424 | bytes 27262976 | tf_op jit(solution)/shard_map/dot_general | solution.py:207
  283.2 11.4 %collective-permute-done.17.a_second = bf16[256,2560]{1,0:T(8,128)(2,1)S(1)} collective-permute-done((bf16[256,2560]{1,0:T(8,128)(2,1)S(1)}, bf16[256,2560]{1,0:T(8,128)(2,1)S(1)}, u32[]{:S(2)}, u32[]{:S(2)}) %collective-permute-start.17) | collective-permute-done | bytes 1310752 | tf_op jit(solution)/shard_map/ppermute | solution.py:134
  294.6 5.9 %collective-permute-done.21.z_first = bf16[256,2560]{1,0:T(8,128)(2,1)S(1)} collective-permute-done((bf16[256,2560]{1,0:T(8,128)(2,1)S(1)}, bf16[256,2560]{1,0:T(8,128)(2,1)S(1)}, u32[]{:S(2)}, u32[]{:S(2)}) %collective-permute-start.21) | collective-permute-done | bytes 1310752 | tf_op jit(solution)/shard_map/ppermute | solution.py:134
  300.5 23.6 %collective-permute-done.23.z_second = bf16[256,2560]{1,0:T(8,128)(2,1)S(1)} collective-permute-done((bf16[256,2560]{1,0:T(8,128)(2,1)S(1)}, bf16[256,2560]{1,0:T(8,128)(2,1)S(1)}, u32[]{:S(2)}, u32[]{:S(2)}) %collective-permute-start.23) | collective-permute-done | bytes 1310752 | tf_op jit(solution)/shard_map/ppermute | solution.py:134
  324.1 7.3 %shard_map.71 = bf16[256,5120]{1,0:T(8,128)(2,1)} custom-call(f32[256,5120]{1,0:T(8,128)} %fusion.5.own, bf16[256,2560]{1,0:T(8,128)(2,1)S(1)} %collective-permute-done.16.a_first, bf16[256,2560]{1,0:T(8,128)(2,1)S(1)} %collective-permute-done.17.a_second, bf16[256,2560]{1,0:T(8,128)(2,1)S(1)} %collective-permute-done.21.z_first, ...), custom_call_target="tpu_custom_call" | custom-call | flops 7864320 | bytes 13107200 | tf_op jit(solution)/shard_map/pallas_call | solution.py:100
  (100 shorter events, 11.9 us)
Async XLA Ops:
  6.5 31.8 %all-gather.2.cloned.1.call-start = ((), (), s32[]{:S(2)}) async-start(), calls=%async_computation | async-start | bytes 6291456 | tf_op jit(solution)/shard_map/all_gather | solution.py:172
  8.8 8.5 %collective-permute-start = (s32[4,40]{1,0:T(4,128)S(1)}, s32[4,40]{1,0:T(4,128)S(1)}, u32[]{:S(2)}, u32[]{:S(2)}) collective-permute-start(s32[4,40]{1,0:T(4,128)S(1)} %broadcast_add_fusion), channel_id=1, source_target_pairs={{0,16},{1,17},{2,18},{3,19},{4,20},{5,21},{6,22},{7,23},{8,24},{9,... | collective-permute-start | bytes 1928 | tf_op jit(solution)/shard_map/ppermute | solution.py:134
  12.9 4.4 %collective-permute-start.1 = (s32[4,40]{1,0:T(4,128)S(1)}, s32[4,40]{1,0:T(4,128)S(1)}, u32[]{:S(2)}, u32[]{:S(2)}) collective-permute-start(s32[4,40]{1,0:T(4,128)S(1)} %broadcast_add_fusion), channel_id=1, source_target_pairs={{0,2},{1,5},{2,0},{3,7},{4,6},{5,1},{6,4},{7,3},{8,10},{9,13},{10,... | collective-permute-start | bytes 1928 | tf_op jit(solution)/shard_map/ppermute | solution.py:134
  14.4 5.4 %collective-permute-start.2 = (s32[4,40]{1,0:T(4,128)S(1)}, s32[4,40]{1,0:T(4,128)S(1)}, u32[]{:S(2)}, u32[]{:S(2)}) collective-permute-start(s32[4,40]{1,0:T(4,128)S(1)} %broadcast_add_fusion), channel_id=1, source_target_pairs={{0,18},{1,21},{2,16},{3,23},{4,22},{5,17},{6,20},{7,19},{8,26},{9,... | collective-permute-start | bytes 1928 | tf_op jit(solution)/shard_map/ppermute | solution.py:134
  23.2 5.6 %copy-start.1 = (bf16[128,3072]{1,0:T(8,128)(2,1)}, bf16[128,3072]{1,0:T(8,128)(2,1)S(1)}, u32[]{:S(2)}) copy-start(bf16[128,3072]{1,0:T(8,128)(2,1)S(1)} %get-tuple-element.33.blocks_ref) | copy-start | bytes 2359300
  23.2 8.9 %copy-start.3 = (bf16[128,3072]{1,0:T(8,128)(2,1)}, bf16[128,3072]{1,0:T(8,128)(2,1)S(1)}, u32[]{:S(2)}) copy-start(bf16[128,3072]{1,0:T(8,128)(2,1)S(1)} %get-tuple-element.34.blocks_ref) | copy-start | bytes 2359300
  23.2 108.5 %copy-start.2 = (bf16[128,3072]{1,0:T(8,128)(2,1)}, bf16[128,3072]{1,0:T(8,128)(2,1)S(1)}, u32[]{:S(2)}) copy-start(bf16[128,3072]{1,0:T(8,128)(2,1)S(1)} %get-tuple-element.35.blocks_ref) | copy-start | bytes 2359300
  23.2 70.4 %collective-permute-start.12 = (bf16[128,3072]{1,0:T(8,128)(2,1)S(1)}, bf16[128,3072]{1,0:T(8,128)(2,1)}, u32[]{:S(2)}, u32[]{:S(2)}) collective-permute-start(bf16[128,3072]{1,0:T(8,128)(2,1)S(1)} %get-tuple-element.33.blocks_ref), channel_id=1, source_target_pairs={{0,16},{1,17},{2,18},{3,19},{4,20},{5,21},{6,22},{7,23},{8,24},{9,... | collective-permute-start | bytes 2359304 | tf_op jit(solution)/shard_map/ppermute | solution.py:134
  23.6 70.0 %collective-permute-start.14 = (bf16[128,3072]{1,0:T(8,128)(2,1)S(1)}, bf16[128,3072]{1,0:T(8,128)(2,1)}, u32[]{:S(2)}, u32[]{:S(2)}) collective-permute-start(bf16[128,3072]{1,0:T(8,128)(2,1)S(1)} %get-tuple-element.33.blocks_ref), channel_id=1, source_target_pairs={{0,2},{1,5},{2,0},{3,7},{4,6},{5,1},{6,4},{7,3},{8,10},{9,13},{10,... | collective-permute-start | bytes 2359304 | tf_op jit(solution)/shard_map/ppermute | solution.py:134
  25.0 102.2 %collective-permute-start.9 = (bf16[128,3072]{1,0:T(8,128)(2,1)S(1)}, bf16[128,3072]{1,0:T(8,128)(2,1)}, u32[]{:S(2)}, u32[]{:S(2)}) collective-permute-start(bf16[128,3072]{1,0:T(8,128)(2,1)S(1)} %get-tuple-element.34.blocks_ref), channel_id=1, source_target_pairs={{0,16},{1,17},{2,18},{3,19},{4,20},{5,21},{6,22},{7,23},{8,24},{9,... | collective-permute-start | bytes 2359304 | tf_op jit(solution)/shard_map/ppermute | solution.py:134
  26.7 104.9 %collective-permute-start.11 = (bf16[128,3072]{1,0:T(8,128)(2,1)S(1)}, bf16[128,3072]{1,0:T(8,128)(2,1)}, u32[]{:S(2)}, u32[]{:S(2)}) collective-permute-start(bf16[128,3072]{1,0:T(8,128)(2,1)S(1)} %get-tuple-element.34.blocks_ref), channel_id=1, source_target_pairs={{0,2},{1,5},{2,0},{3,7},{4,6},{5,1},{6,4},{7,3},{8,10},{9,13},{10,... | collective-permute-start | bytes 2359304 | tf_op jit(solution)/shard_map/ppermute | solution.py:134
  32.0 112.0 %collective-permute-start.6 = (bf16[128,3072]{1,0:T(8,128)(2,1)S(1)}, bf16[128,3072]{1,0:T(8,128)(2,1)S(1)}, u32[]{:S(2)}, u32[]{:S(2)}) collective-permute-start(bf16[128,3072]{1,0:T(8,128)(2,1)S(1)} %get-tuple-element.35.blocks_ref), channel_id=1, source_target_pairs={{0,16},{1,17},{2,18},{3,19},{4,20},{5,21},{6,22},{7,23},{8,24},{9,... | collective-permute-start | bytes 2359304 | tf_op jit(solution)/shard_map/ppermute | solution.py:134
  38.4 90.3 %copy-start = (bf16[256,8192]{1,0:T(8,128)(2,1)S(1)}, bf16[256,8192]{1,0:T(8,128)(2,1)}, u32[]{:S(2)}) copy-start(bf16[256,8192]{1,0:T(8,128)(2,1)} %all-gather.2.cloned.1.call-done) | copy-start | bytes 12582916
  93.5 66.2 %collective-permute-start.3 = (bf16[128,3072]{1,0:T(8,128)(2,1)}, bf16[128,3072]{1,0:T(8,128)(2,1)}, u32[]{:S(2)}, u32[]{:S(2)}) collective-permute-start(bf16[128,3072]{1,0:T(8,128)(2,1)} %get-tuple-element.36.blocks_ref), channel_id=1, source_target_pairs={{0,16},{1,17},{2,18},{3,19},{4,20},{5,21},{6,22},{7,23},{8,24},{9,... | collective-permute-start | bytes 2359304 | tf_op jit(solution)/shard_map/ppermute | solution.py:134
  93.5 67.7 %collective-permute-start.13 = (bf16[128,3072]{1,0:T(8,128)(2,1)}, bf16[128,3072]{1,0:T(8,128)(2,1)S(1)}, u32[]{:S(2)}, u32[]{:S(2)}) collective-permute-start(bf16[128,3072]{1,0:T(8,128)(2,1)} %collective-permute-done.12.blocks_ref), channel_id=1, source_target_pairs={{0,2},{1,5},{2,0},{3,7},{4,6},{5,1},{6,4},{7,3},{8,10},{9,13},{10,... | collective-permute-start | bytes 2359304 | tf_op jit(solution)/shard_map/ppermute | solution.py:134
  127.2 35.7 %collective-permute-start.10 = (bf16[128,3072]{1,0:T(8,128)(2,1)}, bf16[128,3072]{1,0:T(8,128)(2,1)S(1)}, u32[]{:S(2)}, u32[]{:S(2)}) collective-permute-start(bf16[128,3072]{1,0:T(8,128)(2,1)} %collective-permute-done.9.blocks_ref), channel_id=1, source_target_pairs={{0,2},{1,5},{2,0},{3,7},{4,6},{5,1},{6,4},{7,3},{8,10},{9,13},{10,... | collective-permute-start | bytes 2359304 | tf_op jit(solution)/shard_map/ppermute | solution.py:134
  131.7 64.8 %collective-permute-start.8 = (bf16[128,3072]{1,0:T(8,128)(2,1)S(1)}, bf16[128,3072]{1,0:T(8,128)(2,1)S(1)}, u32[]{:S(2)}, u32[]{:S(2)}) collective-permute-start(bf16[128,3072]{1,0:T(8,128)(2,1)S(1)} %get-tuple-element.35.blocks_ref), channel_id=1, source_target_pairs={{0,2},{1,5},{2,0},{3,7},{4,6},{5,1},{6,4},{7,3},{8,10},{9,13},{10,... | collective-permute-start | bytes 2359304 | tf_op jit(solution)/shard_map/ppermute | solution.py:134
  144.0 26.6 %copy-start.12 = (bf16[128,3072]{1,0:T(8,128)(2,1)}, bf16[128,3072]{1,0:T(8,128)(2,1)S(1)}, u32[]{:S(2)}) copy-start(bf16[128,3072]{1,0:T(8,128)(2,1)S(1)} %collective-permute-done.6.blocks_ref) | copy-start | bytes 2359300
  144.0 67.4 %collective-permute-start.5 = (bf16[128,3072]{1,0:T(8,128)(2,1)}, bf16[128,3072]{1,0:T(8,128)(2,1)}, u32[]{:S(2)}, u32[]{:S(2)}) collective-permute-start(bf16[128,3072]{1,0:T(8,128)(2,1)} %get-tuple-element.36.blocks_ref), channel_id=1, source_target_pairs={{0,2},{1,5},{2,0},{3,7},{4,6},{5,1},{6,4},{7,3},{8,10},{9,13},{10,... | collective-permute-start | bytes 2359304 | tf_op jit(solution)/shard_map/ppermute | solution.py:134
  159.8 40.9 %collective-permute-start.7 = (bf16[128,3072]{1,0:T(8,128)(2,1)S(1)}, bf16[128,3072]{1,0:T(8,128)(2,1)S(1)}, u32[]{:S(2)}, u32[]{:S(2)}) collective-permute-start(bf16[128,3072]{1,0:T(8,128)(2,1)S(1)} %collective-permute-done.6.blocks_ref), channel_id=1, source_target_pairs={{0,2},{1,5},{2,0},{3,7},{4,6},{5,1},{6,4},{7,3},{8,10},{9,13},{10,... | collective-permute-start | bytes 2359304 | tf_op jit(solution)/shard_map/ppermute | solution.py:134
  161.3 9.4 %copy-start.14 = (bf16[128,3072]{1,0:T(8,128)(2,1)}, bf16[128,3072]{1,0:T(8,128)(2,1)S(1)}, u32[]{:S(2)}) copy-start(bf16[128,3072]{1,0:T(8,128)(2,1)S(1)} %collective-permute-done.13.blocks_ref) | copy-start | bytes 2359300
  161.3 53.3 %collective-permute-start.4 = (bf16[128,3072]{1,0:T(8,128)(2,1)}, bf16[128,3072]{1,0:T(8,128)(2,1)}, u32[]{:S(2)}, u32[]{:S(2)}) collective-permute-start(bf16[128,3072]{1,0:T(8,128)(2,1)} %collective-permute-done.3.blocks_ref), channel_id=1, source_target_pairs={{0,2},{1,5},{2,0},{3,7},{4,6},{5,1},{6,4},{7,3},{8,10},{9,13},{10,... | collective-permute-start | bytes 2359304 | tf_op jit(solution)/shard_map/ppermute | solution.py:134
  162.9 7.7 %copy-start.13 = (bf16[128,3072]{1,0:T(8,128)(2,1)}, bf16[128,3072]{1,0:T(8,128)(2,1)S(1)}, u32[]{:S(2)}) copy-start(bf16[128,3072]{1,0:T(8,128)(2,1)S(1)} %collective-permute-done.10.blocks_ref) | copy-start | bytes 2359300
  162.9 59.6 %collective-permute-start.19 = (bf16[256,2048]{1,0:T(8,128)(2,1)}, bf16[256,2048]{1,0:T(8,128)(2,1)}, u32[]{:S(2)}, u32[]{:S(2)}) collective-permute-start(bf16[256,2048]{1,0:T(8,128)(2,1)} %pad_maximum_fusion.2), channel_id=1, source_target_pairs={{0,12},{1,11},{2,14},{3,9},{4,8},{5,15},{6,10},{7,13},{8,4},{9,3},... | collective-permute-start | bytes 3145736 | tf_op jit(solution)/shard_map/ppermute | solution.py:134
  196.5 0.9 copy-start.15
  200.7 0.9 copy-start.16
  214.6 3.4 %copy-start.8 = (bf16[256,512]{1,0:T(8,128)(2,1)S(1)}, bf16[256,512]{1,0:T(8,128)(2,1)}, u32[]{:S(2)}) copy-start(bf16[256,512]{1,0:T(8,128)(2,1)} %get-tuple-element.21) | copy-start | bytes 786436
  214.6 3.4 %copy-start.9 = (bf16[256,512]{1,0:T(8,128)(2,1)S(1)}, bf16[256,512]{1,0:T(8,128)(2,1)}, u32[]{:S(2)}) copy-start(bf16[256,512]{1,0:T(8,128)(2,1)} %get-tuple-element.22) | copy-start | bytes 786436
  214.6 3.4 %copy-start.10 = (bf16[256,512]{1,0:T(8,128)(2,1)S(1)}, bf16[256,512]{1,0:T(8,128)(2,1)}, u32[]{:S(2)}) copy-start(bf16[256,512]{1,0:T(8,128)(2,1)} %get-tuple-element.23) | copy-start | bytes 786436
  214.6 3.4 %copy-start.11 = (bf16[256,512]{1,0:T(8,128)(2,1)S(1)}, bf16[256,512]{1,0:T(8,128)(2,1)}, u32[]{:S(2)}) copy-start(bf16[256,512]{1,0:T(8,128)(2,1)} %get-tuple-element.24) | copy-start | bytes 786436
  214.6 5.9 %copy-start.4 = (bf16[256,512]{1,0:T(8,128)(2,1)S(1)}, bf16[256,512]{1,0:T(8,128)(2,1)}, u32[]{:S(2)}) copy-start(bf16[256,512]{1,0:T(8,128)(2,1)} %get-tuple-element.25) | copy-start | bytes 786436
  214.6 5.9 %copy-start.5 = (bf16[256,512]{1,0:T(8,128)(2,1)S(1)}, bf16[256,512]{1,0:T(8,128)(2,1)}, u32[]{:S(2)}) copy-start(bf16[256,512]{1,0:T(8,128)(2,1)} %get-tuple-element.26) | copy-start | bytes 786436
  214.6 5.9 %copy-start.6 = (bf16[256,512]{1,0:T(8,128)(2,1)S(1)}, bf16[256,512]{1,0:T(8,128)(2,1)}, u32[]{:S(2)}) copy-start(bf16[256,512]{1,0:T(8,128)(2,1)} %get-tuple-element.27) | copy-start | bytes 786436
  214.6 5.9 %copy-start.7 = (bf16[256,512]{1,0:T(8,128)(2,1)S(1)}, bf16[256,512]{1,0:T(8,128)(2,1)}, u32[]{:S(2)}) copy-start(bf16[256,512]{1,0:T(8,128)(2,1)} %get-tuple-element.28) | copy-start | bytes 786436
  219.1 26.9 %collective-permute-start.18 = (bf16[256,2048]{1,0:T(8,128)(2,1)}, bf16[256,2048]{1,0:T(8,128)(2,1)}, u32[]{:S(2)}, u32[]{:S(2)}) collective-permute-start(bf16[256,2048]{1,0:T(8,128)(2,1)} %pad_maximum_fusion.1), channel_id=1, source_target_pairs={{0,8},{1,9},{2,10},{3,11},{4,12},{5,13},{6,14},{7,15},{8,0},{9,1},... | collective-permute-start | bytes 3145736 | tf_op jit(solution)/shard_map/ppermute | solution.py:134
  220.5 16.4 %slice-start = ((s8[20971520]{0:T(1024)(128)(4,1)}), s8[4194304]{0:T(1024)(128)(4,1)S(1)}, s32[]{:S(2)}) async-start(s8[20971520]{0:T(1024)(128)(4,1)} %bitcast.56), calls=%async_computation.1 | async-start | bytes 8388608
  221.7 15.2 %slice-start.1 = ((s8[20971520]{0:T(1024)(128)(4,1)}), s8[4194304]{0:T(1024)(128)(4,1)S(1)}, s32[]{:S(2)}) async-start(s8[20971520]{0:T(1024)(128)(4,1)} %bitcast.56), calls=%async_computation.2 | async-start | bytes 8388608
  221.7 15.2 %slice-start.2 = ((s8[20971520]{0:T(1024)(128)(4,1)}), s8[4194304]{0:T(1024)(128)(4,1)S(1)}, s32[]{:S(2)}) async-start(s8[20971520]{0:T(1024)(128)(4,1)} %bitcast.56), calls=%async_computation.3 | async-start | bytes 8388608
  221.7 15.2 %slice-start.3 = ((s8[20971520]{0:T(1024)(128)(4,1)}), s8[4194304]{0:T(1024)(128)(4,1)S(1)}, s32[]{:S(2)}) async-start(s8[20971520]{0:T(1024)(128)(4,1)} %bitcast.56), calls=%async_computation.4 | async-start | bytes 8388608
  221.7 15.2 %slice-start.4 = ((s8[20971520]{0:T(1024)(128)(4,1)}), s8[4194304]{0:T(1024)(128)(4,1)S(1)}, s32[]{:S(2)}) async-start(s8[20971520]{0:T(1024)(128)(4,1)} %bitcast.56), calls=%async_computation.5 | async-start | bytes 8388608
  221.7 15.2 %collective-permute-start.15 = (bf16[256,2048]{1,0:T(8,128)(2,1)}, bf16[256,2048]{1,0:T(8,128)(2,1)}, u32[]{:S(2)}, u32[]{:S(2)}) collective-permute-start(bf16[256,2048]{1,0:T(8,128)(2,1)} %pad_maximum_fusion), channel_id=1, source_target_pairs={{0,4},{1,3},{2,6},{3,1},{4,0},{5,7},{6,2},{7,5},{8,12},{9,11},{10,... | collective-permute-start | bytes 3145736 | tf_op jit(solution)/shard_map/ppermute | solution.py:134
  234.7 21.6 %collective-permute-start.20 = (bf16[256,2560]{1,0:T(8,128)(2,1)}, bf16[256,2560]{1,0:T(8,128)(2,1)S(1)}, u32[]{:S(2)}, u32[]{:S(2)}) collective-permute-start(bf16[256,2560]{1,0:T(8,128)(2,1)} %get-tuple-element.38), channel_id=1, source_target_pairs={{0,4},{1,3},{2,6},{3,1},{4,0},{5,7},{6,2},{7,5},{8,12},{9,11},{10,... | collective-permute-start | bytes 3932168 | tf_op jit(solution)/shard_map/ppermute | solution.py:134
  236.0 30.7 %collective-permute-start.22 = (bf16[256,2560]{1,0:T(8,128)(2,1)S(1)}, bf16[256,2560]{1,0:T(8,128)(2,1)}, u32[]{:S(2)}, u32[]{:S(2)}) collective-permute-start(bf16[256,2560]{1,0:T(8,128)(2,1)S(1)} %get-tuple-element.37), channel_id=1, source_target_pairs={{0,4},{1,3},{2,6},{3,1},{4,0},{5,7},{6,2},{7,5},{8,12},{9,11},{10,... | collective-permute-start | bytes 3932168 | tf_op jit(solution)/shard_map/ppermute | solution.py:134
  244.0 39.2 %collective-permute-start.16 = (bf16[256,2560]{1,0:T(8,128)(2,1)S(1)}, bf16[256,2560]{1,0:T(8,128)(2,1)S(1)}, u32[]{:S(2)}, u32[]{:S(2)}) collective-permute-start(bf16[256,2560]{1,0:T(8,128)(2,1)S(1)} %get-tuple-element.40), channel_id=1, source_target_pairs={{0,4},{1,3},{2,6},{3,1},{4,0},{5,7},{6,2},{7,5},{8,12},{9,11},{10,... | collective-permute-start | bytes 3932168 | tf_op jit(solution)/shard_map/ppermute | solution.py:134
  245.2 49.5 %collective-permute-start.17 = (bf16[256,2560]{1,0:T(8,128)(2,1)S(1)}, bf16[256,2560]{1,0:T(8,128)(2,1)S(1)}, u32[]{:S(2)}, u32[]{:S(2)}) collective-permute-start(bf16[256,2560]{1,0:T(8,128)(2,1)S(1)} %get-tuple-element.39), channel_id=1, source_target_pairs={{0,4},{1,3},{2,6},{3,1},{4,0},{5,7},{6,2},{7,5},{8,12},{9,11},{10,... | collective-permute-start | bytes 3932168 | tf_op jit(solution)/shard_map/ppermute | solution.py:134
  256.2 14.6 %copy-start.17 = (bf16[256,512]{1,0:T(8,128)(2,1)S(1)}, bf16[256,512]{1,0:T(8,128)(2,1)}, u32[]{:S(2)}) copy-start(bf16[256,512]{1,0:T(8,128)(2,1)} %get-tuple-element.29) | copy-start | bytes 786436
  256.2 14.6 %copy-start.18 = (bf16[256,512]{1,0:T(8,128)(2,1)S(1)}, bf16[256,512]{1,0:T(8,128)(2,1)}, u32[]{:S(2)}) copy-start(bf16[256,512]{1,0:T(8,128)(2,1)} %get-tuple-element.30) | copy-start | bytes 786436
  256.2 14.6 %copy-start.19 = (bf16[256,512]{1,0:T(8,128)(2,1)S(1)}, bf16[256,512]{1,0:T(8,128)(2,1)}, u32[]{:S(2)}) copy-start(bf16[256,512]{1,0:T(8,128)(2,1)} %get-tuple-element.31) | copy-start | bytes 786436
  256.2 14.6 %copy-start.20 = (bf16[256,512]{1,0:T(8,128)(2,1)S(1)}, bf16[256,512]{1,0:T(8,128)(2,1)}, u32[]{:S(2)}) copy-start(bf16[256,512]{1,0:T(8,128)(2,1)} %get-tuple-element.32) | copy-start | bytes 786436
  268.7 31.8 %collective-permute-start.21 = (bf16[256,2560]{1,0:T(8,128)(2,1)S(1)}, bf16[256,2560]{1,0:T(8,128)(2,1)S(1)}, u32[]{:S(2)}, u32[]{:S(2)}) collective-permute-start(bf16[256,2560]{1,0:T(8,128)(2,1)S(1)} %get-tuple-element.16), channel_id=1, source_target_pairs={{0,8},{1,9},{2,10},{3,11},{4,12},{5,13},{6,14},{7,15},{8,0},{9,1},... | collective-permute-start | bytes 3932168 | tf_op jit(solution)/shard_map/ppermute | solution.py:134
  269.1 55.0 %collective-permute-start.23 = (bf16[256,2560]{1,0:T(8,128)(2,1)S(1)}, bf16[256,2560]{1,0:T(8,128)(2,1)S(1)}, u32[]{:S(2)}, u32[]{:S(2)}) collective-permute-start(bf16[256,2560]{1,0:T(8,128)(2,1)S(1)} %get-tuple-element.15), channel_id=1, source_target_pairs={{0,8},{1,9},{2,10},{3,11},{4,12},{5,13},{6,14},{7,15},{8,0},{9,1},... | collective-permute-start | bytes 3932168 | tf_op jit(solution)/shard_map/ppermute | solution.py:134
Sparse Core Ops, SparseCore 0:
  8.9 16.4 all-gather.1

commit v3 on v2

--- a/solution.py
+++ b/solution.py
@@ -155,19 +155,6 @@
     tied = lax.optimization_barrier([kept_blocks] + slots_from)
     kept_blocks, slots_from = tied[0], tied[1:]
 
-    order = []
-    for row in range(rows_here):
-        chunk = kept_blocks[row * BS : (row + 1) * BS]
-        held = {(0, 0): chunk}
-        for masks in across:
-            for known in list(held):
-                held[(known[0] ^ masks[0], known[1] ^ masks[1])] = swap(held[known], masks)
-        for known in list(held):
-            held[(known[0] ^ weight_bit[0], known[1] ^ weight_bit[1])] = swap(
-                held[known], weight_bit
-            )
-        order += [(row, masks, held[masks]) for masks in offsets]
-
     gathered, gain_all = (
         lax.all_gather(tokens, "tensor", axis=1, tiled=True),
         lax.all_gather(norm_gain, "tensor", axis=0, tiled=True),
@@ -191,35 +178,68 @@
     x_a = swap(features_of(me ^ mine(sum_bit)), sum_bit)
     x_own = features_of(me)
 
-    dense = None
     slot_table = dict(zip(offsets, slots_from))
-    for row, masks, blocks in order:
-        peer = me ^ mine(masks)
+
+    def put(masks, row, blocks, dense):
         where = jnp.concatenate(
             [
-                (position(peer) * rows_here + row).reshape(1).astype(jnp.int32),
-                slot_table[masks][row],
+                (position(me ^ mine(masks)) * rows_here + row).reshape(1).astype(jnp.int32),
+                slot_table[masks][row : row + blocks.shape[0] // BS].reshape(-1),
             ]
         )
-        dense = place(where, blocks, dense, group * shard_rows, column_blocks)
+        return place(where, blocks, dense, group * shard_rows, column_blocks)
+
+    def plus(masks, more):
+        return (masks[0] ^ more[0], masks[1] ^ more[1])
+
+    near = swap(kept_blocks, weight_bit)
+    chunks = []
+    for row in range(rows_here):
+        held = {(0, 0): kept_blocks[row * BS : (row + 1) * BS]}
+        for masks in across:
+            for known in list(held):
+                held[plus(known, masks)] = swap(held[known], masks)
+        del held[(0, 0)]
+        chunks.append(held)
+    dense = put((0, 0), 0, kept_blocks, None)
+    late = []
+    tie = [x_far, x_z, x_a]
+    for row, held in enumerate(chunks):
+        names = list(held)
+        tied = lax.optimization_barrier([held[name] for name in names] + tie + [dense])
+        if row == 0:
+            x_far, x_z, x_a = tied[-4:-1]
+        dense = tied[-1]
+        tie = []
+        if row == 1 or rows_here == 1:
+            dense = put(weight_bit, 0, near, dense)
+        for masks, blocks, row_of in late:
+            dense = put(masks, row_of, blocks, dense)
+        late = []
+        for name, blocks in zip(names, tied):
+            late.append((plus(name, weight_bit), swap(blocks, weight_bit), row))
+            dense = put(name, row, blocks, dense)
+    for masks, blocks, row_of in late:
+        dense = put(masks, row_of, blocks, dense)
 
     def product(left):
         return jnp.dot(left, dense, preferred_element_type=jnp.float32)
 
     half = column_blocks * BS // 2
     far = product(x_far).astype(jnp.bfloat16)
+    far, x_z, x_a = lax.optimization_barrier((far, x_z, x_a))
     far_first = swap(far[:, :half], sum_bit)
     far_second = swap(far[:, half:], sum_bit)
     part_z = product(x_z)
+    part_z, x_a, x_own = lax.optimization_barrier((part_z, x_a, x_own))
     part_a = product(x_a).astype(jnp.bfloat16)
     a_first = swap(part_a[:, :half], sum_bit)
     a_second = swap(part_a[:, half:], sum_bit)
-    z_first = swap(
-        (part_z[:, :half] + far_first.astype(jnp.float32)).astype(jnp.bfloat16), z_bit
-    )
-    z_second = swap(
-        (part_z[:, half:] + far_second.astype(jnp.float32)).astype(jnp.bfloat16), z_bit
-    )
+    sum_first = (part_z[:, :half] + far_first.astype(jnp.float32)).astype(jnp.bfloat16)
+    sum_first, far_second = lax.optimization_barrier((sum_first, far_second))
+    z_first = swap(sum_first, z_bit)
+    sum_second = (part_z[:, half:] + far_second.astype(jnp.float32)).astype(jnp.bfloat16)
+    z_second = swap(sum_second, z_bit)
     return finish(product(x_own), a_first, a_second, z_first, z_second)
 
 

time: 339 us -> 314 us (0.926)
  Pallas kernels: 59.2 us -> 45.4 us
  waiting for transfers between devices: 165 us -> 155 us
  other arithmetic: 21.9 us -> 16.8 us
    pallas_call x16 -> x10, Pallas kernels: 51.9 us -> 38.2 us  [place(): pl.pallas_call(functools.partial(place_body, slots=slots, column_blocks=c...]
    ppermute x24 -> x21, waiting for transfers between devices: 164 us -> 154 us  [swap(): return lax.ppermute(value, ('dp', 'tensor'), pairs)]
    concatenate x16 -> x10, other arithmetic: 9.68 us -> 6.07 us  [put(): jnp.concatenate([(position(me ^ mine(masks)) * rows_here + row).reshape(1...]
    ppermute x24 -> x21, starting transfers between devices: 27.8 us -> 27.4 us  [swap(): return lax.ppermute(value, ('dp', 'tensor'), pairs)]
  transfers between devices with their start and end apart: 25 -> 22, of which waited for: 10 -> 13; matrix products, arithmetic and copies ran while one was open for 20% -> 14% of each run, Pallas kernels for 15% -> 11%
where the time goes in v3:
time: 314 us; the launch traced here: 313 us
  waiting for transfers between devices  155 us (49%)
  Pallas kernels  45.4 us (14%)
  matrix products  42.9 us (14%)
  starting transfers between devices  27.4 us (9%)
  other arithmetic  16.8 us (5%)
  between operations  13.7 us (4%)
  local copies, waits for them, and re-layouts  9.38 us (3%)
    ppermute x21, waiting for transfers between devices, swap(): return lax.ppermute(value, ('dp', 'tensor'), pairs)  154 us
    dot_general x4, matrix products, product(): return jnp.dot(left, dense, preferred_element_type=jnp.float32)  42.9 us
    pallas_call x10, Pallas kernels, place(): pl.pallas_call(functools.partial(place_body, slots=slots, column_blocks=c...  38.2 us
    ppermute x21, starting transfers between devices, swap(): return lax.ppermute(value, ('dp', 'tensor'), pairs)  27.4 us
    pallas_call x1, Pallas kernels, finish(): pl.pallas_call(functools.partial(finish_body, steps=steps, heads=heads),...  7.29 us
  transfers between devices with their start and end apart: 22, of which 13 were waited for; matrix products, arithmetic and copies ran while one was open for 14% of the time, Pallas kernels for 11%

profile of v3, /device:TPU:0, one launch (start us, length us, event | category | flops | bytes accessed | tf_op | source)
XLA Modules:
  0.0 312.9 jit_solution(17341756646376240185)
XLA Ops:
  6.5 0.7 all-gather.2.cloned.1.call-update
  7.3 0.7 iota_compare_fusion.1
  8.0 0.8 select_reduce_fusion
  8.8 4.1 %collective-permute-start = (s32[4,40]{1,0:T(4,128)S(1)}, s32[4,40]{1,0:T(4,128)S(1)}, u32[]{:S(2)}, u32[]{:S(2)}) collective-permute-start(s32[4,40]{1,0:T(4,128)S(1)} %broadcast_add_fusion), channel_id=1, source_target_pairs={{0,16},{1,17},{2,18},{3,19},{4,20},{5,21},{6,22},{7,23},{8,24},{9,... | collective-permute-start | bytes 1928 | tf_op jit(solution)/shard_map/ppermute | solution.py:134
  12.9 1.5 collective-permute-start.1
  14.4 2.0 all_gather.7
  16.6 3.2 %collective-permute-done.2 = s32[4,40]{1,0:T(4,128)S(1)} collective-permute-done((s32[4,40]{1,0:T(4,128)S(1)}, s32[4,40]{1,0:T(4,128)S(1)}, u32[]{:S(2)}, u32[]{:S(2)}) %collective-permute-start.2) | collective-permute-done | bytes 672 | tf_op jit(solution)/shard_map/ppermute | solution.py:134
  20.3 3.9 %fusion.5 = (bf16[128,3072]{1,0:T(8,128)(2,1)}, bf16[128,3072]{1,0:T(8,128)(2,1)}, bf16[128,3072]{1,0:T(8,128)(2,1)}, bf16[128,3072]{1,0:T(8,128)(2,1)}) fusion(bf16[512,3072]{1,0:T(8,128)(2,1)} %blocks_ref), kind=kLoop, calls=%fused_computation.61 | loop fusion | bytes 6291456 | tf_op jit(solution)/shard_map/slice | solution.py:198
  24.2 0.8 collective-permute-start.3
  25.3 3.3 %fusion = f32[256]{0:T(256)S(1)} fusion(bf16[256,8192]{1,0:T(8,128)(2,1)} %all-gather.2.cloned.1.call-done), kind=kLoop, calls=%fused_computation.2 | loop fusion | flops 6291200 | bytes 4195328 | tf_op jit(solution)/shard_map/reduce_sum | solution.py:163
  28.8 1.2 fusion.2
  29.9 1.3 constant_dynamic-slice_fusion.3
  31.3 1.2 pad_maximum_fusion
  32.4 2.7 collective-permute-start.4
  35.1 1.1 pad_maximum_fusion.1
  36.8 1.1 pad_maximum_fusion.2
  38.2 21.7 %collective-permute-done.3.blocks_ref = bf16[128,3072]{1,0:T(8,128)(2,1)} collective-permute-done((bf16[128,3072]{1,0:T(8,128)(2,1)}, bf16[128,3072]{1,0:T(8,128)(2,1)}, u32[]{:S(2)}, u32[]{:S(2)}) %collective-permute-start.3) | collective-permute-done | bytes 786464 | tf_op jit(solution)/shard_map/ppermute | solution.py:134
  60.0 0.7 pad_add_fusion.where_ref
  60.6 6.2 %shard_map.55.rest_0_ = bf16[2048,5120]{1,0:T(8,128)(2,1)} custom-call(s32[161]{0:T(256)} %pad_add_fusion.where_ref, bf16[512,3072]{1,0:T(8,128)(2,1)} %blocks_ref), custom_call_target="tpu_custom_call" | custom-call | bytes 8388608 | tf_op jit(solution)/shard_map/pallas_call | solution.py:41
  66.8 25.0 %collective-permute-done.4 = bf16[256,2048]{1,0:T(8,128)(2,1)} collective-permute-done((bf16[256,2048]{1,0:T(8,128)(2,1)}, bf16[256,2048]{1,0:T(8,128)(2,1)}, u32[]{:S(2)}, u32[]{:S(2)}) %collective-permute-start.4) | collective-permute-done | bytes 1048608 | tf_op jit(solution)/shard_map/ppermute | solution.py:134
  91.8 3.1 collective-permute-start.8
  94.9 19.5 %collective-permute-done.5 = bf16[256,2048]{1,0:T(8,128)(2,1)} collective-permute-done((bf16[256,2048]{1,0:T(8,128)(2,1)}, bf16[256,2048]{1,0:T(8,128)(2,1)}, u32[]{:S(2)}, u32[]{:S(2)}) %collective-permute-start.5) | collective-permute-done | bytes 1048608 | tf_op jit(solution)/shard_map/ppermute | solution.py:134
  114.8 0.6 pad_add_fusion.5.where_ref
  115.4 3.2 %shard_map.56.rest_0_ = bf16[2048,5120]{1,0:T(8,128)(2,1)} custom-call(s32[41]{0:T(128)} %pad_add_fusion.5.where_ref, bf16[128,3072]{1,0:T(8,128)(2,1)} %collective-permute-done.3.blocks_ref, bf16[2048,5120]{1,0:T(8,128)(2,1)} %shard_map.55.rest_0_), custom_call_target="tpu_custom_call", output_to_operand_aliasing={{}: (2, {})} | custom-call | bytes 2097152 | tf_op jit(solution)/shard_map/pallas_call | solution.py:41
  118.6 1.7 collective-permute-start.12
  120.3 2.4 collective-permute-start.7
  122.8 0.6 pad_add_fusion.3.where_ref
  123.4 0.6 pad_add_fusion.4.where_ref
  124.0 0.6 pad_add_fusion.6.where_ref
  124.6 0.6 pad_add_fusion.7.where_ref
  125.2 0.6 pad_add_fusion.1.where_ref
  125.9 1.7 copy-done.1
  127.5 6.0 %shard_map.57.rest_0_ = bf16[2048,5120]{1,0:T(8,128)(2,1)} custom-call(s32[161]{0:T(256)} %pad_add_fusion.1.where_ref, bf16[512,3072]{1,0:T(8,128)(2,1)} %copy-done.1, bf16[2048,5120]{1,0:T(8,128)(2,1)} %shard_map.56.rest_0_), custom_call_target="tpu_custom_call", output_to_operand_aliasing={{}: (2, {})} | custom-call | bytes 8388608 | tf_op jit(solution)/shard_map/pallas_call | solution.py:41
  133.6 3.2 %shard_map.58.rest_0_ = bf16[2048,5120]{1,0:T(8,128)(2,1)} custom-call(s32[41]{0:T(128)} %pad_add_fusion.6.where_ref, bf16[128,3072]{1,0:T(8,128)(2,1)} %collective-permute-done.10.blocks_ref, bf16[2048,5120]{1,0:T(8,128)(2,1)} %shard_map.57.rest_0_), custom_call_target="tpu_custom_call", output_to_operand_aliasing={{}: (2, {})} | custom-call | bytes 2097152 | tf_op jit(solution)/shard_map/pallas_call | solution.py:41
  136.8 3.3 %shard_map.59.rest_0_ = bf16[2048,5120]{1,0:T(8,128)(2,1)} custom-call(s32[41]{0:T(128)} %pad_add_fusion.4.where_ref, bf16[128,3072]{1,0:T(8,128)(2,1)} %collective-permute-done.9.blocks_ref, bf16[2048,5120]{1,0:T(8,128)(2,1)} %shard_map.58.rest_0_), custom_call_target="tpu_custom_call", output_to_operand_aliasing={{}: (2, {})} | custom-call | bytes 2097152 | tf_op jit(solution)/shard_map/pallas_call | solution.py:41
  140.0 16.4 %collective-permute-done.8.blocks_ref = bf16[128,3072]{1,0:T(8,128)(2,1)} collective-permute-done((bf16[128,3072]{1,0:T(8,128)(2,1)}, bf16[128,3072]{1,0:T(8,128)(2,1)}, u32[]{:S(2)}, u32[]{:S(2)}) %collective-permute-start.8) | collective-permute-done | bytes 786464 | tf_op jit(solution)/shard_map/ppermute | solution.py:134
  156.4 1.5 collective-permute-start.14
  157.9 3.3 %shard_map.60.rest_0_ = bf16[2048,5120]{1,0:T(8,128)(2,1)} custom-call(s32[41]{0:T(128)} %pad_add_fusion.7.where_ref, bf16[128,3072]{1,0:T(8,128)(2,1)} %collective-permute-done.12.blocks_ref, bf16[2048,5120]{1,0:T(8,128)(2,1)} %shard_map.59.rest_0_), custom_call_target="tpu_custom_call", output_to_operand_aliasing={{}: (2, {})} | custom-call | bytes 2097152 | tf_op jit(solution)/shard_map/pallas_call | solution.py:41
  161.2 3.3 %shard_map.61.rest_0_ = bf16[2048,5120]{1,0:T(8,128)(2,1)} custom-call(s32[41]{0:T(128)} %pad_add_fusion.3.where_ref, bf16[128,3072]{1,0:T(8,128)(2,1)} %collective-permute-done.8.blocks_ref, bf16[2048,5120]{1,0:T(8,128)(2,1)} %shard_map.60.rest_0_), custom_call_target="tpu_custom_call", output_to_operand_aliasing={{}: (2, {})} | custom-call | bytes 2097152 | tf_op jit(solution)/shard_map/pallas_call | solution.py:41
  164.5 8.7 %collective-permute-done.7.blocks_ref = bf16[128,3072]{1,0:T(8,128)(2,1)} collective-permute-done((bf16[128,3072]{1,0:T(8,128)(2,1)}, bf16[128,3072]{1,0:T(8,128)(2,1)}, u32[]{:S(2)}, u32[]{:S(2)}) %collective-permute-start.7) | collective-permute-done | bytes 786464 | tf_op jit(solution)/shard_map/ppermute | solution.py:134
  173.2 1.5 collective-permute-start.13
  175.9 0.6 pad_add_fusion.8.where_ref
  176.5 0.6 pad_add_fusion.9.where_ref
  177.3 0.9 copy-done.5
  178.2 3.2 %shard_map.62.rest_0_ = bf16[2048,5120]{1,0:T(8,128)(2,1)} custom-call(s32[41]{0:T(128)} %pad_add_fusion.9.where_ref, bf16[128,3072]{1,0:T(8,128)(2,1)} %copy-done.5, bf16[2048,5120]{1,0:T(8,128)(2,1)} %shard_map.61.rest_0_), custom_call_target="tpu_custom_call", output_to_operand_aliasing={{}: (2, {})} | custom-call | bytes 2097152 | tf_op jit(solution)/shard_map/pallas_call | solution.py:41
  181.4 3.2 %shard_map.63.rest_0_ = bf16[2048,5120]{1,0:T(8,128)(2,1)} custom-call(s32[41]{0:T(128)} %pad_add_fusion.8.where_ref, bf16[128,3072]{1,0:T(8,128)(2,1)} %collective-permute-done.7.blocks_ref, bf16[2048,5120]{1,0:T(8,128)(2,1)} %shard_map.62.rest_0_), custom_call_target="tpu_custom_call", output_to_operand_aliasing={{}: (2, {})} | custom-call | bytes 2097152 | tf_op jit(solution)/shard_map/pallas_call | solution.py:41
  184.6 0.8 collective-permute-done.13.blocks_ref
  185.4 0.9 copy-done.6
  186.3 3.2 %shard_map.64 = bf16[2048,5120]{1,0:T(8,128)(2,1)} custom-call(s32[41]{0:T(128)} %pad_add_fusion.2.where_ref, bf16[128,3072]{1,0:T(8,128)(2,1)} %copy-done.6, bf16[2048,5120]{1,0:T(8,128)(2,1)} %shard_map.63.rest_0_), custom_call_target="tpu_custom_call", output_to_operand_aliasing={{}: (2, {})} | custom-call | bytes 2097152 | tf_op jit(solution)/shard_map/pallas_call | solution.py:41
  189.5 10.1 %convolution_convert_fusion.1 = bf16[256,5120]{1,0:T(8,128)(2,1)S(1)} fusion(bf16[256,2048]{1,0:T(8,128)(2,1)} %collective-permute-done.4, bf16[2048,5120]{1,0:T(8,128)(2,1)} %shard_map.64), kind=kOutput, calls=%fused_computation.6 | convolution fusion | flops 5370019840 | bytes 24641536 | tf_op jit(solution)/shard_map/dot_general | solution.py:226
  199.6 10.2 %fusion.8 = f32[256,5120]{1,0:T(8,128)S(1)} fusion(bf16[256,2048]{1,0:T(8,128)(2,1)} %collective-permute-done.5, bf16[2048,5120]{1,0:T(8,128)(2,1)} %shard_map.64), kind=kOutput, calls=%fused_computation.64 | convolution fusion | flops 5368709120 | bytes 27262976 | tf_op jit(solution)/shard_map/dot_general | solution.py:226
  210.0 1.5 collective-permute-start.17
  211.5 10.4 %convolution_convert_fusion = bf16[256,5120]{1,0:T(8,128)(2,1)S(1)} fusion(bf16[256,2048]{1,0:T(8,128)(2,1)} %collective-permute-done.6, bf16[2048,5120]{1,0:T(8,128)(2,1)} %shard_map.64), kind=kOutput, calls=%fused_computation.5 | convolution fusion | flops 5370019840 | bytes 24641536 | tf_op jit(solution)/shard_map/dot_general | solution.py:226
  221.9 0.6 collective-permute-start.18
  222.7 1.5 collective-permute-start.15
  224.2 0.6 collective-permute-start.16
  224.8 2.9 collective-permute-done.17
  228.0 13.7 %collective-permute-done.18 = bf16[256,2560]{1,0:T(8,128)(2,1)S(1)} collective-permute-done((bf16[256,2560]{1,0:T(8,128)(2,1)S(1)}, bf16[256,2560]{1,0:T(8,128)(2,1)S(1)}, u32[]{:S(2)}, u32[]{:S(2)}) %collective-permute-start.18) | collective-permute-done | bytes 1310752 | tf_op jit(solution)/shard_map/ppermute | solution.py:134
  242.0 2.1 collective-permute-start.20
  244.1 12.2 %fusion.9.own = f32[256,5120]{1,0:T(8,128)} fusion(bf16[256,2048]{1,0:T(8,128)(2,1)S(1)} %pad_maximum_fusion.3, bf16[2048,5120]{1,0:T(8,128)(2,1)} %shard_map.64), kind=kOutput, calls=%fused_computation.65 | convolution fusion | flops 5368709120 | bytes 27262976 | tf_op jit(solution)/shard_map/dot_general | solution.py:226
  256.3 13.5 %collective-permute-done.16.a_second = bf16[256,2560]{1,0:T(8,128)(2,1)S(1)} collective-permute-done((bf16[256,2560]{1,0:T(8,128)(2,1)S(1)}, bf16[256,2560]{1,0:T(8,128)(2,1)S(1)}, u32[]{:S(2)}, u32[]{:S(2)}) %collective-permute-start.16) | collective-permute-done | bytes 1310752 | tf_op jit(solution)/shard_map/ppermute | solution.py:134
  269.8 3.6 %collective-permute-done.19.z_first = bf16[256,2560]{1,0:T(8,128)(2,1)S(1)} collective-permute-done((bf16[256,2560]{1,0:T(8,128)(2,1)S(1)}, bf16[256,2560]{1,0:T(8,128)(2,1)S(1)}, u32[]{:S(2)}, u32[]{:S(2)}) %collective-permute-start.19) | collective-permute-done | bytes 1310752 | tf_op jit(solution)/shard_map/ppermute | solution.py:134
  273.4 25.4 %collective-permute-done.20.z_second = bf16[256,2560]{1,0:T(8,128)(2,1)S(1)} collective-permute-done((bf16[256,2560]{1,0:T(8,128)(2,1)S(1)}, bf16[256,2560]{1,0:T(8,128)(2,1)S(1)}, u32[]{:S(2)}, u32[]{:S(2)}) %collective-permute-start.20) | collective-permute-done | bytes 1310752 | tf_op jit(solution)/shard_map/ppermute | solution.py:134
  298.8 7.3 %shard_map.65 = bf16[256,5120]{1,0:T(8,128)(2,1)} custom-call(f32[256,5120]{1,0:T(8,128)} %fusion.9.own, bf16[256,2560]{1,0:T(8,128)(2,1)S(1)} %collective-permute-done.15.a_first, bf16[256,2560]{1,0:T(8,128)(2,1)S(1)} %collective-permute-done.16.a_second, bf16[256,2560]{1,0:T(8,128)(2,1)S(1)} %collective-permute-done.19.z_first, ...), custom_call_target="tpu_custom_call" | custom-call | flops 7864320 | bytes 13107200 | tf_op jit(solution)/shard_map/pallas_call | solution.py:100
  (46 shorter events, 4.8 us)
Async XLA Ops:
  6.5 18.8 %all-gather.2.cloned.1.call-start = ((), (), s32[]{:S(2)}) async-start(), calls=%async_computation | async-start | bytes 6291456 | tf_op jit(solution)/shard_map/all_gather | solution.py:159
  8.8 7.8 %collective-permute-start = (s32[4,40]{1,0:T(4,128)S(1)}, s32[4,40]{1,0:T(4,128)S(1)}, u32[]{:S(2)}, u32[]{:S(2)}) collective-permute-start(s32[4,40]{1,0:T(4,128)S(1)} %broadcast_add_fusion), channel_id=1, source_target_pairs={{0,16},{1,17},{2,18},{3,19},{4,20},{5,21},{6,22},{7,23},{8,24},{9,... | collective-permute-start | bytes 1928 | tf_op jit(solution)/shard_map/ppermute | solution.py:134
  12.9 3.7 %collective-permute-start.1 = (s32[4,40]{1,0:T(4,128)S(1)}, s32[4,40]{1,0:T(4,128)S(1)}, u32[]{:S(2)}, u32[]{:S(2)}) collective-permute-start(s32[4,40]{1,0:T(4,128)S(1)} %broadcast_add_fusion), channel_id=1, source_target_pairs={{0,2},{1,5},{2,0},{3,7},{4,6},{5,1},{6,4},{7,3},{8,10},{9,13},{10,... | collective-permute-start | bytes 1928 | tf_op jit(solution)/shard_map/ppermute | solution.py:134
  14.4 5.4 %collective-permute-start.2 = (s32[4,40]{1,0:T(4,128)S(1)}, s32[4,40]{1,0:T(4,128)S(1)}, u32[]{:S(2)}, u32[]{:S(2)}) collective-permute-start(s32[4,40]{1,0:T(4,128)S(1)} %broadcast_add_fusion), channel_id=1, source_target_pairs={{0,18},{1,21},{2,16},{3,23},{4,22},{5,17},{6,20},{7,19},{8,26},{9,... | collective-permute-start | bytes 1928 | tf_op jit(solution)/shard_map/ppermute | solution.py:134
  19.8 106.1 %collective-permute-start.11 = (bf16[512,3072]{1,0:T(8,128)(2,1)}, bf16[512,3072]{1,0:T(8,128)(2,1)S(1)}, u32[]{:S(2)}, u32[]{:S(2)}) collective-permute-start(bf16[512,3072]{1,0:T(8,128)(2,1)} %blocks_ref), channel_id=1, source_target_pairs={{0,2},{1,5},{2,0},{3,7},{4,6},{5,1},{6,4},{7,3},{8,10},{9,13},{10,... | collective-permute-start | bytes 9437192 | tf_op jit(solution)/shard_map/ppermute | solution.py:134
  24.2 35.7 %collective-permute-start.3 = (bf16[128,3072]{1,0:T(8,128)(2,1)}, bf16[128,3072]{1,0:T(8,128)(2,1)}, u32[]{:S(2)}, u32[]{:S(2)}) collective-permute-start(bf16[128,3072]{1,0:T(8,128)(2,1)} %get-tuple-element.72), channel_id=1, source_target_pairs={{0,16},{1,17},{2,18},{3,19},{4,20},{5,21},{6,22},{7,23},{8,24},{9,... | collective-permute-start | bytes 2359304 | tf_op jit(solution)/shard_map/ppermute | solution.py:134
  25.3 3.4 %copy-start = (bf16[256,8192]{1,0:T(8,128)(2,1)S(1)}, bf16[256,8192]{1,0:T(8,128)(2,1)}, u32[]{:S(2)}) copy-start(bf16[256,8192]{1,0:T(8,128)(2,1)} %all-gather.2.cloned.1.call-done) | copy-start | bytes 12582916
  32.4 59.4 %collective-permute-start.4 = (bf16[256,2048]{1,0:T(8,128)(2,1)}, bf16[256,2048]{1,0:T(8,128)(2,1)}, u32[]{:S(2)}, u32[]{:S(2)}) collective-permute-start(bf16[256,2048]{1,0:T(8,128)(2,1)} %pad_maximum_fusion), channel_id=1, source_target_pairs={{0,12},{1,11},{2,14},{3,9},{4,8},{5,15},{6,10},{7,13},{8,4},{9,3},... | collective-permute-start | bytes 3145736 | tf_op jit(solution)/shard_map/ppermute | solution.py:134
  36.2 78.2 %collective-permute-start.5 = (bf16[256,2048]{1,0:T(8,128)(2,1)}, bf16[256,2048]{1,0:T(8,128)(2,1)}, u32[]{:S(2)}, u32[]{:S(2)}) collective-permute-start(bf16[256,2048]{1,0:T(8,128)(2,1)} %pad_maximum_fusion.1), channel_id=1, source_target_pairs={{0,8},{1,9},{2,10},{3,11},{4,12},{5,13},{6,14},{7,15},{8,0},{9,1},... | collective-permute-start | bytes 3145736 | tf_op jit(solution)/shard_map/ppermute | solution.py:134
  37.9 76.6 %collective-permute-start.6 = (bf16[256,2048]{1,0:T(8,128)(2,1)}, bf16[256,2048]{1,0:T(8,128)(2,1)}, u32[]{:S(2)}, u32[]{:S(2)}) collective-permute-start(bf16[256,2048]{1,0:T(8,128)(2,1)} %pad_maximum_fusion.2), channel_id=1, source_target_pairs={{0,4},{1,3},{2,6},{3,1},{4,0},{5,7},{6,2},{7,5},{8,12},{9,11},{10,... | collective-permute-start | bytes 3145736 | tf_op jit(solution)/shard_map/ppermute | solution.py:134
  59.9 58.7 %collective-permute-start.9 = (bf16[128,3072]{1,0:T(8,128)(2,1)}, bf16[128,3072]{1,0:T(8,128)(2,1)}, u32[]{:S(2)}, u32[]{:S(2)}) collective-permute-start(bf16[128,3072]{1,0:T(8,128)(2,1)} %get-tuple-element.69), channel_id=1, source_target_pairs={{0,16},{1,17},{2,18},{3,19},{4,20},{5,21},{6,22},{7,23},{8,24},{9,... | collective-permute-start | bytes 2359304 | tf_op jit(solution)/shard_map/ppermute | solution.py:134
  91.8 64.6 %collective-permute-start.8 = (bf16[128,3072]{1,0:T(8,128)(2,1)}, bf16[128,3072]{1,0:T(8,128)(2,1)}, u32[]{:S(2)}, u32[]{:S(2)}) collective-permute-start(bf16[128,3072]{1,0:T(8,128)(2,1)} %get-tuple-element.70), channel_id=1, source_target_pairs={{0,16},{1,17},{2,18},{3,19},{4,20},{5,21},{6,22},{7,23},{8,24},{9,... | collective-permute-start | bytes 2359304 | tf_op jit(solution)/shard_map/ppermute | solution.py:134
  114.5 19.1 %collective-permute-start.10 = (bf16[128,3072]{1,0:T(8,128)(2,1)}, bf16[128,3072]{1,0:T(8,128)(2,1)}, u32[]{:S(2)}, u32[]{:S(2)}) collective-permute-start(bf16[128,3072]{1,0:T(8,128)(2,1)} %collective-permute-done.3.blocks_ref), channel_id=1, source_target_pairs={{0,2},{1,5},{2,0},{3,7},{4,6},{5,1},{6,4},{7,3},{8,10},{9,13},{10,... | collective-permute-start | bytes 2359304 | tf_op jit(solution)/shard_map/ppermute | solution.py:134
  118.6 39.3 %collective-permute-start.12 = (bf16[128,3072]{1,0:T(8,128)(2,1)}, bf16[128,3072]{1,0:T(8,128)(2,1)}, u32[]{:S(2)}, u32[]{:S(2)}) collective-permute-start(bf16[128,3072]{1,0:T(8,128)(2,1)} %collective-permute-done.9.blocks_ref), channel_id=1, source_target_pairs={{0,2},{1,5},{2,0},{3,7},{4,6},{5,1},{6,4},{7,3},{8,10},{9,13},{10,... | collective-permute-start | bytes 2359304 | tf_op jit(solution)/shard_map/ppermute | solution.py:134
  120.3 52.9 %collective-permute-start.7 = (bf16[128,3072]{1,0:T(8,128)(2,1)}, bf16[128,3072]{1,0:T(8,128)(2,1)}, u32[]{:S(2)}, u32[]{:S(2)}) collective-permute-start(bf16[128,3072]{1,0:T(8,128)(2,1)} %get-tuple-element.71), channel_id=1, source_target_pairs={{0,16},{1,17},{2,18},{3,19},{4,20},{5,21},{6,22},{7,23},{8,24},{9,... | collective-permute-start | bytes 2359304 | tf_op jit(solution)/shard_map/ppermute | solution.py:134
  125.9 1.7 copy-start.1
  156.4 20.8 %collective-permute-start.14 = (bf16[128,3072]{1,0:T(8,128)(2,1)}, bf16[128,3072]{1,0:T(8,128)(2,1)S(1)}, u32[]{:S(2)}, u32[]{:S(2)}) collective-permute-start(bf16[128,3072]{1,0:T(8,128)(2,1)} %collective-permute-done.8.blocks_ref), channel_id=1, source_target_pairs={{0,2},{1,5},{2,0},{3,7},{4,6},{5,1},{6,4},{7,3},{8,10},{9,13},{10,... | collective-permute-start | bytes 2359304 | tf_op jit(solution)/shard_map/ppermute | solution.py:134
  161.2 15.9 %copy-start.2 = (bf16[256,512]{1,0:T(8,128)(2,1)S(1)}, bf16[256,512]{1,0:T(8,128)(2,1)}, u32[]{:S(2)}) copy-start(bf16[256,512]{1,0:T(8,128)(2,1)} %get-tuple-element.54) | copy-start | bytes 786436
  161.2 15.9 %copy-start.3 = (bf16[256,512]{1,0:T(8,128)(2,1)S(1)}, bf16[256,512]{1,0:T(8,128)(2,1)}, u32[]{:S(2)}) copy-start(bf16[256,512]{1,0:T(8,128)(2,1)} %get-tuple-element.55) | copy-start | bytes 786436
  161.2 15.9 %copy-start.4 = (bf16[256,512]{1,0:T(8,128)(2,1)S(1)}, bf16[256,512]{1,0:T(8,128)(2,1)}, u32[]{:S(2)}) copy-start(bf16[256,512]{1,0:T(8,128)(2,1)} %get-tuple-element.56) | copy-start | bytes 786436
  173.2 12.2 %collective-permute-start.13 = (bf16[128,3072]{1,0:T(8,128)(2,1)}, bf16[128,3072]{1,0:T(8,128)(2,1)S(1)}, u32[]{:S(2)}, u32[]{:S(2)}) collective-permute-start(bf16[128,3072]{1,0:T(8,128)(2,1)} %collective-permute-done.7.blocks_ref), channel_id=1, source_target_pairs={{0,2},{1,5},{2,0},{3,7},{4,6},{5,1},{6,4},{7,3},{8,10},{9,13},{10,... | collective-permute-start | bytes 2359304 | tf_op jit(solution)/shard_map/ppermute | solution.py:134
  177.3 0.9 copy-start.5
  185.4 0.9 copy-start.6
  210.0 17.7 %collective-permute-start.17 = (bf16[256,2560]{1,0:T(8,128)(2,1)S(1)}, bf16[256,2560]{1,0:T(8,128)(2,1)S(1)}, u32[]{:S(2)}, u32[]{:S(2)}) collective-permute-start(bf16[256,2560]{1,0:T(8,128)(2,1)S(1)} %get-tuple-element.74), channel_id=1, source_target_pairs={{0,4},{1,3},{2,6},{3,1},{4,0},{5,7},{6,2},{7,5},{8,12},{9,11},{10,... | collective-permute-start | bytes 3932168 | tf_op jit(solution)/shard_map/ppermute | solution.py:134
  221.9 19.8 %collective-permute-start.18 = (bf16[256,2560]{1,0:T(8,128)(2,1)S(1)}, bf16[256,2560]{1,0:T(8,128)(2,1)S(1)}, u32[]{:S(2)}, u32[]{:S(2)}) collective-permute-start(bf16[256,2560]{1,0:T(8,128)(2,1)S(1)} %get-tuple-element.73), channel_id=1, source_target_pairs={{0,4},{1,3},{2,6},{3,1},{4,0},{5,7},{6,2},{7,5},{8,12},{9,11},{10,... | collective-permute-start | bytes 3932168 | tf_op jit(solution)/shard_map/ppermute | solution.py:134
  222.7 33.6 %collective-permute-start.15 = (bf16[256,2560]{1,0:T(8,128)(2,1)S(1)}, bf16[256,2560]{1,0:T(8,128)(2,1)S(1)}, u32[]{:S(2)}, u32[]{:S(2)}) collective-permute-start(bf16[256,2560]{1,0:T(8,128)(2,1)S(1)} %get-tuple-element.76), channel_id=1, source_target_pairs={{0,4},{1,3},{2,6},{3,1},{4,0},{5,7},{6,2},{7,5},{8,12},{9,11},{10,... | collective-permute-start | bytes 3932168 | tf_op jit(solution)/shard_map/ppermute | solution.py:134
  224.2 45.6 %collective-permute-start.16 = (bf16[256,2560]{1,0:T(8,128)(2,1)S(1)}, bf16[256,2560]{1,0:T(8,128)(2,1)S(1)}, u32[]{:S(2)}, u32[]{:S(2)}) collective-permute-start(bf16[256,2560]{1,0:T(8,128)(2,1)S(1)} %get-tuple-element.75), channel_id=1, source_target_pairs={{0,4},{1,3},{2,6},{3,1},{4,0},{5,7},{6,2},{7,5},{8,12},{9,11},{10,... | collective-permute-start | bytes 3932168 | tf_op jit(solution)/shard_map/ppermute | solution.py:134
  241.7 31.7 %collective-permute-start.19 = (bf16[256,2560]{1,0:T(8,128)(2,1)S(1)}, bf16[256,2560]{1,0:T(8,128)(2,1)S(1)}, u32[]{:S(2)}, u32[]{:S(2)}) collective-permute-start(bf16[256,2560]{1,0:T(8,128)(2,1)S(1)} %add_convert_fusion.1), channel_id=1, source_target_pairs={{0,8},{1,9},{2,10},{3,11},{4,12},{5,13},{6,14},{7,15},{8,0},{9,1},... | collective-permute-start | bytes 3932168 | tf_op jit(solution)/shard_map/ppermute | solution.py:134
  242.0 56.8 %collective-permute-start.20 = (bf16[256,2560]{1,0:T(8,128)(2,1)S(1)}, bf16[256,2560]{1,0:T(8,128)(2,1)S(1)}, u32[]{:S(2)}, u32[]{:S(2)}) collective-permute-start(bf16[256,2560]{1,0:T(8,128)(2,1)S(1)} %add_convert_fusion), channel_id=1, source_target_pairs={{0,8},{1,9},{2,10},{3,11},{4,12},{5,13},{6,14},{7,15},{8,0},{9,1},... | collective-permute-start | bytes 3932168 | tf_op jit(solution)/shard_map/ppermute | solution.py:134
Sparse Core Ops, SparseCore 0:
  8.9 16.3 all-gather.1

commit v4 on v3

--- a/solution.py
+++ b/solution.py
@@ -173,10 +173,9 @@
             parts.append(lax.dynamic_slice_in_dim(normed, owner * shard_rows, shard_rows, 1))
         return jnp.concatenate(parts, axis=1)
 
-    x_far = swap(features_of(me ^ mine(far_bits)), far_bits)
-    x_z = swap(features_of(me ^ 4), z_bit)
-    x_a = swap(features_of(me ^ mine(sum_bit)), sum_bit)
+    sends = [features_of(me ^ mine(masks)) for masks in (far_bits, z_bit, sum_bit)]
     x_own = features_of(me)
+    x_far, x_z, x_a = [swap(v, m) for v, m in zip(sends, (far_bits, z_bit, sum_bit))]
 
     slot_table = dict(zip(offsets, slots_from))
 
@@ -194,24 +193,19 @@
 
     near = swap(kept_blocks, weight_bit)
     chunks = []
-    for row in range(rows_here):
-        held = {(0, 0): kept_blocks[row * BS : (row + 1) * BS]}
-        for masks in across:
-            for known in list(held):
-                held[plus(known, masks)] = swap(held[known], masks)
-        del held[(0, 0)]
-        chunks.append(held)
+    held = {(0, 0): kept_blocks}
+    for masks in across:
+        for known in list(held):
+            held[plus(known, masks)] = swap(held[known], masks)
+    del held[(0, 0)]
+    chunks.append(held)
     dense = put((0, 0), 0, kept_blocks, None)
     late = []
-    tie = [x_far, x_z, x_a]
     for row, held in enumerate(chunks):
         names = list(held)
-        tied = lax.optimization_barrier([held[name] for name in names] + tie + [dense])
+        tied = lax.optimization_barrier([held[name] for name in names] + [dense])
+        dense = tied[-1]
         if row == 0:
-            x_far, x_z, x_a = tied[-4:-1]
-        dense = tied[-1]
-        tie = []
-        if row == 1 or rows_here == 1:
             dense = put(weight_bit, 0, near, dense)
         for masks, blocks, row_of in late:
             dense = put(masks, row_of, blocks, dense)
@@ -227,12 +221,12 @@
 
     half = column_blocks * BS // 2
     far = product(x_far).astype(jnp.bfloat16)
-    far, x_z, x_a = lax.optimization_barrier((far, x_z, x_a))
     far_first = swap(far[:, :half], sum_bit)
     far_second = swap(far[:, half:], sum_bit)
-    part_z = product(x_z)
-    part_z, x_a, x_own = lax.optimization_barrier((part_z, x_a, x_own))
-    part_a = product(x_a).astype(jnp.bfloat16)
+    far, x_z, x_a, x_own = lax.optimization_barrier((far, x_z, x_a, x_own))
+    both = product(jnp.concatenate([x_z, x_a], axis=0))
+    part_z = both[: x_z.shape[0]]
+    part_a = both[x_z.shape[0] :].astype(jnp.bfloat16)
     a_first = swap(part_a[:, :half], sum_bit)
     a_second = swap(part_a[:, half:], sum_bit)
     sum_first = (part_z[:, :half] + far_first.astype(jnp.float32)).astype(jnp.bfloat16)

time: 314 us -> 338 us (1.076)
  waiting for transfers between devices: 155 us -> 214 us
  Pallas kernels: 45.4 us -> 31.3 us
  starting transfers between devices: 27.4 us -> 17.7 us
  local copies, waits for them, and re-layouts: 9.38 us -> 3.13 us
    ppermute x21 -> x15, waiting for transfers between devices: 154 us -> 213 us  [swap(): return lax.ppermute(value, ('dp', 'tensor'), pairs)]
    pallas_call x10 -> x4, Pallas kernels: 38.2 us -> 24 us  [place(): pl.pallas_call(functools.partial(place_body, slots=slots, column_blocks=c...]
    ppermute x21 -> x15, starting transfers between devices: 27.4 us -> 17.7 us  [swap(): return lax.ppermute(value, ('dp', 'tensor'), pairs)]
    slice x1 -> x0, local copies, waits for them, and re-layouts: 3.9 us -> none  [per_device(): held = {(0, 0): kept_blocks[row * BS:(row + 1) * BS]}]
    concatenate x10 -> x4, other arithmetic: 6.07 us -> 2.56 us  [put(): jnp.concatenate([(position(me ^ mine(masks)) * rows_here + row).reshape(1...]
    unnamed x14 -> x4, local copies, waits for them, and re-layouts: 3.61 us -> 0.19 us
    dot_general x4 -> x3, matrix products: 42.9 us -> 41.2 us  [product(): return jnp.dot(left, dense, preferred_element_type=jnp.float32)]
  transfers between devices with their start and end apart: 22 -> 16, of which waited for: 13 -> 8; matrix products, arithmetic and copies ran while one was open for 14% -> 17% of each run, Pallas kernels for 11% -> 7%
where the time goes in v4:
time: 338 us; the launch traced here: 337 us
  waiting for transfers between devices  214 us (63%)
  matrix products  41.2 us (12%)
  Pallas kernels  31.3 us (9%)
  starting transfers between devices  17.7 us (5%)
  other arithmetic  14.1 us (4%)
  between operations  13.7 us (4%)
    ppermute x15, waiting for transfers between devices, swap(): return lax.ppermute(value, ('dp', 'tensor'), pairs)  213 us
    dot_general x3, matrix products, product(): return jnp.dot(left, dense, preferred_element_type=jnp.float32)  41.2 us
    pallas_call x4, Pallas kernels, place(): pl.pallas_call(functools.partial(place_body, slots=slots, column_blocks=c...  24 us
    ppermute x15, starting transfers between devices, swap(): return lax.ppermute(value, ('dp', 'tensor'), pairs)  17.7 us
    pallas_call x1, Pallas kernels, finish(): pl.pallas_call(functools.partial(finish_body, steps=steps, heads=heads),...  7.29 us
  transfers between devices with their start and end apart: 16, of which 8 were waited for; matrix products, arithmetic and copies ran while one was open for 17% of the time, Pallas kernels for 7%

profile of v4, /device:TPU:0, one launch (start us, length us, event | category | flops | bytes accessed | tf_op | source)
XLA Modules:
  0.0 337.2 jit_solution(2462478631462149804)
XLA Ops:
  6.5 0.7 all-gather.2.cloned.1.call-update
  7.3 0.9 iota_compare_fusion.1
  8.2 0.8 select_reduce_fusion
  9.0 4.1 %collective-permute-start.1 = (s32[4,40]{1,0:T(4,128)S(1)}, s32[4,40]{1,0:T(4,128)S(1)}, u32[]{:S(2)}, u32[]{:S(2)}) collective-permute-start(s32[4,40]{1,0:T(4,128)S(1)} %broadcast_add_fusion), channel_id=1, source_target_pairs={{0,16},{1,17},{2,18},{3,19},{4,20},{5,21},{6,22},{7,23},{8,24},{9,... | collective-permute-start | bytes 1928 | tf_op jit(solution)/shard_map/ppermute | solution.py:134
  13.1 1.5 collective-permute-start.2
  14.6 0.0 collective-permute-start.3
  14.7 0.0 collective-permute-done.1
  14.7 2.0 collective-permute-done.2
  16.7 3.3 collective-permute-done.3
  20.0 0.3 collective-permute-start.4
  20.3 2.0 all_gather.7
  22.5 0.5 fusion.10
  23.0 0.1 pad_maximum_fusion.4
  23.1 0.3 collective-permute-start.6
  23.5 0.1 reshape.76
  23.6 0.6 pad_add_fusion.1.where_ref
  24.2 6.0 %shard_map.55.rest_0_ = bf16[2048,5120]{1,0:T(8,128)(2,1)} custom-call(s32[161]{0:T(256)} %pad_add_fusion.1.where_ref, bf16[512,3072]{1,0:T(8,128)(2,1)} %blocks_ref), custom_call_target="tpu_custom_call" | custom-call | bytes 8388608 | tf_op jit(solution)/shard_map/pallas_call | solution.py:41
  30.2 0.1 reshape.80
  30.3 0.1 reshape.78
  30.4 0.1 reshape.74
  30.4 126.3 %collective-permute-done.4.blocks_ref = bf16[512,3072]{1,0:T(8,128)(2,1)} collective-permute-done((bf16[512,3072]{1,0:T(8,128)(2,1)}, bf16[512,3072]{1,0:T(8,128)(2,1)}, u32[]{:S(2)}, u32[]{:S(2)}) %collective-permute-start.4) | collective-permute-done | bytes 3145760 | tf_op jit(solution)/shard_map/ppermute | solution.py:134
  156.8 1.5 collective-permute-start.5
  158.3 3.3 fusion
  161.5 0.2 copy-done
  161.7 1.2 fusion.2
  162.9 0.6 constant_dynamic-slice_fusion.3
  163.5 0.1 pad_maximum_fusion
  163.6 0.1 collective-permute-start
  163.7 0.6 pad_add_fusion.3.where_ref
  164.3 0.7 pad_add_fusion.2.where_ref
  165.0 0.6 pad_add_fusion.where_ref
  165.6 0.0 collective-permute-done.6.blocks_ref
  165.6 6.0 %shard_map.56.rest_0_ = bf16[2048,5120]{1,0:T(8,128)(2,1)} custom-call(s32[161]{0:T(256)} %pad_add_fusion.3.where_ref, bf16[512,3072]{1,0:T(8,128)(2,1)} %collective-permute-done.6.blocks_ref, bf16[2048,5120]{1,0:T(8,128)(2,1)} %shard_map.55.rest_0_), custom_call_target="tpu_custom_call", output_to_operand_aliasing={{}: (2, {})} | custom-call | bytes 8388608 | tf_op jit(solution)/shard_map/pallas_call | solution.py:41
  171.6 6.0 %shard_map.57.rest_0_ = bf16[2048,5120]{1,0:T(8,128)(2,1)} custom-call(s32[161]{0:T(256)} %pad_add_fusion.2.where_ref, bf16[512,3072]{1,0:T(8,128)(2,1)} %collective-permute-done.4.blocks_ref, bf16[2048,5120]{1,0:T(8,128)(2,1)} %shard_map.56.rest_0_), custom_call_target="tpu_custom_call", output_to_operand_aliasing={{}: (2, {})} | custom-call | bytes 8388608 | tf_op jit(solution)/shard_map/pallas_call | solution.py:41
  177.6 0.1 pad_maximum_fusion.1
  177.7 2.0 collective-permute-start.7
  179.7 0.1 pad_maximum_fusion.2
  179.9 1.6 collective-permute-start.8
  181.4 0.1 pad_maximum_fusion.3
  181.6 35.3 %collective-permute-done.5.blocks_ref = bf16[512,3072]{1,0:T(8,128)(2,1)} collective-permute-done((bf16[512,3072]{1,0:T(8,128)(2,1)}, bf16[512,3072]{1,0:T(8,128)(2,1)}, u32[]{:S(2)}, u32[]{:S(2)}) %collective-permute-start.5) | collective-permute-done | bytes 3145760 | tf_op jit(solution)/shard_map/ppermute | solution.py:134
  216.8 6.0 %shard_map.58 = bf16[2048,5120]{1,0:T(8,128)(2,1)} custom-call(s32[161]{0:T(256)} %pad_add_fusion.where_ref, bf16[512,3072]{1,0:T(8,128)(2,1)} %collective-permute-done.5.blocks_ref, bf16[2048,5120]{1,0:T(8,128)(2,1)} %shard_map.57.rest_0_), custom_call_target="tpu_custom_call", output_to_operand_aliasing={{}: (2, {})} | custom-call | bytes 8388608 | tf_op jit(solution)/shard_map/pallas_call | solution.py:41
  222.8 0.0 collective-permute-done
  222.8 10.1 %convolution_convert_fusion = bf16[256,5120]{1,0:T(8,128)(2,1)S(1)} fusion(bf16[256,2048]{1,0:T(8,128)(2,1)} %collective-permute-done, bf16[2048,5120]{1,0:T(8,128)(2,1)} %shard_map.58), kind=kOutput, calls=%fused_computation.5 | convolution fusion | flops 5370019840 | bytes 24641536 | tf_op jit(solution)/shard_map/dot_general | solution.py:220
  233.0 0.2 fusion.13
  233.2 0.0 collective-permute-done.7
  233.2 0.0 collective-permute-done.8
  233.2 0.6 collective-permute-start.11
  233.8 1.5 collective-permute-start.12
  235.3 18.8 %fusion.14 = (bf16[512,5120]{1,0:T(8,128)(2,1)}, f32[512,5120]{1,0:T(8,128)}) fusion(bf16[2048,5120]{1,0:T(8,128)(2,1)} %shard_map.58, bf16[256,2048]{1,0:T(8,128)(2,1)} %collective-permute-done.8, bf16[256,2048]{1,0:T(8,128)(2,1)} %collective-permute-done.7), kind=kOutput, calls=%fused_computation.55 | convolution fusion | flops 10744233984 | bytes 38797312 | tf_op jit(solution)/shard_map/dot_general | solution.py:220
  254.1 1.9 fusion.12
  255.9 0.6 collective-permute-start.10
  256.5 1.5 collective-permute-start.9
  258.0 0.0 collective-permute-done.11
  258.0 2.1 fusion.4
  260.1 4.8 %collective-permute-done.12 = bf16[256,2560]{1,0:T(8,128)(2,1)S(1)} collective-permute-done((bf16[256,2560]{1,0:T(8,128)(2,1)S(1)}, bf16[256,2560]{1,0:T(8,128)(2,1)S(1)}, u32[]{:S(2)}, u32[]{:S(2)}) %collective-permute-start.12) | collective-permute-done | bytes 1310752 | tf_op jit(solution)/shard_map/ppermute | solution.py:134
  264.9 2.1 fusion.3
  267.0 0.1 collective-permute-start.14
  267.1 2.0 collective-permute-start.13
  269.1 12.3 %fusion.15.own = f32[256,5120]{1,0:T(8,128)} fusion(bf16[256,2048]{1,0:T(8,128)(2,1)S(1)} %pad_maximum_fusion.3, bf16[2048,5120]{1,0:T(8,128)(2,1)} %shard_map.58), kind=kOutput, calls=%fused_computation.56 | convolution fusion | flops 5368709120 | bytes 27262976 | tf_op jit(solution)/shard_map/dot_general | solution.py:220
  281.3 0.0 collective-permute-done.10.a_second
  281.3 11.7 %collective-permute-done.9.a_first = bf16[256,2560]{1,0:T(8,128)(2,1)S(1)} collective-permute-done((bf16[256,2560]{1,0:T(8,128)(2,1)S(1)}, bf16[256,2560]{1,0:T(8,128)(2,1)S(1)}, u32[]{:S(2)}, u32[]{:S(2)}) %collective-permute-start.9) | collective-permute-done | bytes 1310752 | tf_op jit(solution)/shard_map/ppermute | solution.py:134
  293.0 5.8 %collective-permute-done.14.z_second = bf16[256,2560]{1,0:T(8,128)(2,1)S(1)} collective-permute-done((bf16[256,2560]{1,0:T(8,128)(2,1)S(1)}, bf16[256,2560]{1,0:T(8,128)(2,1)S(1)}, u32[]{:S(2)}, u32[]{:S(2)}) %collective-permute-start.14) | collective-permute-done | bytes 1310752 | tf_op jit(solution)/shard_map/ppermute | solution.py:134
  298.8 24.3 %collective-permute-done.13.z_first = bf16[256,2560]{1,0:T(8,128)(2,1)S(1)} collective-permute-done((bf16[256,2560]{1,0:T(8,128)(2,1)S(1)}, bf16[256,2560]{1,0:T(8,128)(2,1)S(1)}, u32[]{:S(2)}, u32[]{:S(2)}) %collective-permute-start.13) | collective-permute-done | bytes 1310752 | tf_op jit(solution)/shard_map/ppermute | solution.py:134
  323.1 7.3 %shard_map.59 = bf16[256,5120]{1,0:T(8,128)(2,1)} custom-call(f32[256,5120]{1,0:T(8,128)} %fusion.15.own, bf16[256,2560]{1,0:T(8,128)(2,1)S(1)} %collective-permute-done.9.a_first, bf16[256,2560]{1,0:T(8,128)(2,1)S(1)} %collective-permute-done.10.a_second, bf16[256,2560]{1,0:T(8,128)(2,1)S(1)} %collective-permute-done.13.z_first, ...), custom_call_target="tpu_custom_call" | custom-call | flops 7864320 | bytes 13107200 | tf_op jit(solution)/shard_map/pallas_call | solution.py:100
  (11 shorter events, 0.0 us)
Async XLA Ops:
  6.5 16.6 %copy-start.1 = (bf16[512,3072]{1,0:T(8,128)(2,1)S(1)}, bf16[512,3072]{1,0:T(8,128)(2,1)}, u32[]{:S(2)}) copy-start(bf16[512,3072]{1,0:T(8,128)(2,1)} %blocks_ref) | copy-start | bytes 9437188
  6.5 151.7 %all-gather.2.cloned.1.call-start = ((), (), s32[]{:S(2)}) async-start(), calls=%async_computation | async-start | bytes 6291456 | tf_op jit(solution)/shard_map/all_gather | solution.py:159
  9.0 5.7 %collective-permute-start.1 = (s32[4,40]{1,0:T(4,128)S(1)}, s32[4,40]{1,0:T(4,128)S(1)}, u32[]{:S(2)}, u32[]{:S(2)}) collective-permute-start(s32[4,40]{1,0:T(4,128)S(1)} %broadcast_add_fusion), channel_id=1, source_target_pairs={{0,16},{1,17},{2,18},{3,19},{4,20},{5,21},{6,22},{7,23},{8,24},{9,... | collective-permute-start | bytes 1928 | tf_op jit(solution)/shard_map/ppermute | solution.py:134
  13.1 3.6 %collective-permute-start.2 = (s32[4,40]{1,0:T(4,128)S(1)}, s32[4,40]{1,0:T(4,128)S(1)}, u32[]{:S(2)}, u32[]{:S(2)}) collective-permute-start(s32[4,40]{1,0:T(4,128)S(1)} %broadcast_add_fusion), channel_id=1, source_target_pairs={{0,2},{1,5},{2,0},{3,7},{4,6},{5,1},{6,4},{7,3},{8,10},{9,13},{10,... | collective-permute-start | bytes 1928 | tf_op jit(solution)/shard_map/ppermute | solution.py:134
  14.6 5.4 %collective-permute-start.3 = (s32[4,40]{1,0:T(4,128)S(1)}, s32[4,40]{1,0:T(4,128)S(1)}, u32[]{:S(2)}, u32[]{:S(2)}) collective-permute-start(s32[4,40]{1,0:T(4,128)S(1)} %broadcast_add_fusion), channel_id=1, source_target_pairs={{0,18},{1,21},{2,16},{3,23},{4,22},{5,17},{6,20},{7,19},{8,26},{9,... | collective-permute-start | bytes 1928 | tf_op jit(solution)/shard_map/ppermute | solution.py:134
  20.0 136.8 %collective-permute-start.4 = (bf16[512,3072]{1,0:T(8,128)(2,1)}, bf16[512,3072]{1,0:T(8,128)(2,1)}, u32[]{:S(2)}, u32[]{:S(2)}) collective-permute-start(bf16[512,3072]{1,0:T(8,128)(2,1)} %blocks_ref), channel_id=1, source_target_pairs={{0,16},{1,17},{2,18},{3,19},{4,20},{5,21},{6,22},{7,23},{8,24},{9,... | collective-permute-start | bytes 9437192 | tf_op jit(solution)/shard_map/ppermute | solution.py:134
  23.1 142.5 %collective-permute-start.6 = (bf16[512,3072]{1,0:T(8,128)(2,1)S(1)}, bf16[512,3072]{1,0:T(8,128)(2,1)}, u32[]{:S(2)}, u32[]{:S(2)}) collective-permute-start(bf16[512,3072]{1,0:T(8,128)(2,1)S(1)} %copy-done.1), channel_id=1, source_target_pairs={{0,2},{1,5},{2,0},{3,7},{4,6},{5,1},{6,4},{7,3},{8,10},{9,13},{10,... | collective-permute-start | bytes 9437192 | tf_op jit(solution)/shard_map/ppermute | solution.py:134
  156.8 60.1 %collective-permute-start.5 = (bf16[512,3072]{1,0:T(8,128)(2,1)}, bf16[512,3072]{1,0:T(8,128)(2,1)}, u32[]{:S(2)}, u32[]{:S(2)}) collective-permute-start(bf16[512,3072]{1,0:T(8,128)(2,1)} %collective-permute-done.4.blocks_ref), channel_id=1, source_target_pairs={{0,2},{1,5},{2,0},{3,7},{4,6},{5,1},{6,4},{7,3},{8,10},{9,13},{10,... | collective-permute-start | bytes 9437192 | tf_op jit(solution)/shard_map/ppermute | solution.py:134
  158.3 3.4 %copy-start = (bf16[256,8192]{1,0:T(8,128)(2,1)S(1)}, bf16[256,8192]{1,0:T(8,128)(2,1)}, u32[]{:S(2)}) copy-start(bf16[256,8192]{1,0:T(8,128)(2,1)} %all-gather.2.cloned.1.call-done) | copy-start | bytes 12582916
  163.6 59.2 %collective-permute-start = (bf16[256,2048]{1,0:T(8,128)(2,1)S(1)}, bf16[256,2048]{1,0:T(8,128)(2,1)}, u32[]{:S(2)}, u32[]{:S(2)}) collective-permute-start(bf16[256,2048]{1,0:T(8,128)(2,1)S(1)} %pad_maximum_fusion), channel_id=1, source_target_pairs={{0,12},{1,11},{2,14},{3,9},{4,8},{5,15},{6,10},{7,13},{8,4},{9,3},... | collective-permute-start | bytes 3145736 | tf_op jit(solution)/shard_map/ppermute | solution.py:134
  177.7 55.4 %collective-permute-start.7 = (bf16[256,2048]{1,0:T(8,128)(2,1)S(1)}, bf16[256,2048]{1,0:T(8,128)(2,1)}, u32[]{:S(2)}, u32[]{:S(2)}) collective-permute-start(bf16[256,2048]{1,0:T(8,128)(2,1)S(1)} %pad_maximum_fusion.1), channel_id=1, source_target_pairs={{0,8},{1,9},{2,10},{3,11},{4,12},{5,13},{6,14},{7,15},{8,0},{9,1},... | collective-permute-start | bytes 3145736 | tf_op jit(solution)/shard_map/ppermute | solution.py:134
  179.9 53.3 %collective-permute-start.8 = (bf16[256,2048]{1,0:T(8,128)(2,1)S(1)}, bf16[256,2048]{1,0:T(8,128)(2,1)}, u32[]{:S(2)}, u32[]{:S(2)}) collective-permute-start(bf16[256,2048]{1,0:T(8,128)(2,1)S(1)} %pad_maximum_fusion.2), channel_id=1, source_target_pairs={{0,4},{1,3},{2,6},{3,1},{4,0},{5,7},{6,2},{7,5},{8,12},{9,11},{10,... | collective-permute-start | bytes 3145736 | tf_op jit(solution)/shard_map/ppermute | solution.py:134
  233.2 24.9 %collective-permute-start.11 = (bf16[256,2560]{1,0:T(8,128)(2,1)S(1)}, bf16[256,2560]{1,0:T(8,128)(2,1)S(1)}, u32[]{:S(2)}, u32[]{:S(2)}) collective-permute-start(bf16[256,2560]{1,0:T(8,128)(2,1)S(1)} %get-tuple-element.48), channel_id=1, source_target_pairs={{0,4},{1,3},{2,6},{3,1},{4,0},{5,7},{6,2},{7,5},{8,12},{9,11},{10,... | collective-permute-start | bytes 3932168 | tf_op jit(solution)/shard_map/ppermute | solution.py:134
  233.8 31.1 %collective-permute-start.12 = (bf16[256,2560]{1,0:T(8,128)(2,1)S(1)}, bf16[256,2560]{1,0:T(8,128)(2,1)S(1)}, u32[]{:S(2)}, u32[]{:S(2)}) collective-permute-start(bf16[256,2560]{1,0:T(8,128)(2,1)S(1)} %get-tuple-element.47), channel_id=1, source_target_pairs={{0,4},{1,3},{2,6},{3,1},{4,0},{5,7},{6,2},{7,5},{8,12},{9,11},{10,... | collective-permute-start | bytes 3932168 | tf_op jit(solution)/shard_map/ppermute | solution.py:134
  255.9 25.4 %collective-permute-start.10 = (bf16[256,2560]{1,0:T(8,128)(2,1)S(1)}, bf16[256,2560]{1,0:T(8,128)(2,1)S(1)}, u32[]{:S(2)}, u32[]{:S(2)}) collective-permute-start(bf16[256,2560]{1,0:T(8,128)(2,1)S(1)} %get-tuple-element.29), channel_id=1, source_target_pairs={{0,4},{1,3},{2,6},{3,1},{4,0},{5,7},{6,2},{7,5},{8,12},{9,11},{10,... | collective-permute-start | bytes 3932168 | tf_op jit(solution)/shard_map/ppermute | solution.py:134
  256.5 36.5 %collective-permute-start.9 = (bf16[256,2560]{1,0:T(8,128)(2,1)S(1)}, bf16[256,2560]{1,0:T(8,128)(2,1)S(1)}, u32[]{:S(2)}, u32[]{:S(2)}) collective-permute-start(bf16[256,2560]{1,0:T(8,128)(2,1)S(1)} %get-tuple-element.30), channel_id=1, source_target_pairs={{0,4},{1,3},{2,6},{3,1},{4,0},{5,7},{6,2},{7,5},{8,12},{9,11},{10,... | collective-permute-start | bytes 3932168 | tf_op jit(solution)/shard_map/ppermute | solution.py:134
  267.0 31.8 %collective-permute-start.14 = (bf16[256,2560]{1,0:T(8,128)(2,1)S(1)}, bf16[256,2560]{1,0:T(8,128)(2,1)S(1)}, u32[]{:S(2)}, u32[]{:S(2)}) collective-permute-start(bf16[256,2560]{1,0:T(8,128)(2,1)S(1)} %fusion.3), channel_id=1, source_target_pairs={{0,8},{1,9},{2,10},{3,11},{4,12},{5,13},{6,14},{7,15},{8,0},{9,1},... | collective-permute-start | bytes 3932168 | tf_op jit(solution)/shard_map/ppermute | solution.py:134
  267.1 56.0 %collective-permute-start.13 = (bf16[256,2560]{1,0:T(8,128)(2,1)S(1)}, bf16[256,2560]{1,0:T(8,128)(2,1)S(1)}, u32[]{:S(2)}, u32[]{:S(2)}) collective-permute-start(bf16[256,2560]{1,0:T(8,128)(2,1)S(1)} %fusion.4), channel_id=1, source_target_pairs={{0,8},{1,9},{2,10},{3,11},{4,12},{5,13},{6,14},{7,15},{8,0},{9,1},... | collective-permute-start | bytes 3932168 | tf_op jit(solution)/shard_map/ppermute | solution.py:134
Sparse Core Ops, SparseCore 0:
  8.9 16.3 all-gather.1

commit v5 on v3

--- a/solution.py
+++ b/solution.py
@@ -173,10 +173,9 @@
             parts.append(lax.dynamic_slice_in_dim(normed, owner * shard_rows, shard_rows, 1))
         return jnp.concatenate(parts, axis=1)
 
-    x_far = swap(features_of(me ^ mine(far_bits)), far_bits)
-    x_z = swap(features_of(me ^ 4), z_bit)
-    x_a = swap(features_of(me ^ mine(sum_bit)), sum_bit)
+    sends = [features_of(me ^ mine(masks)) for masks in (far_bits, z_bit, sum_bit)]
     x_own = features_of(me)
+    x_far, x_z, x_a = [swap(v, m) for v, m in zip(sends, (far_bits, z_bit, sum_bit))]
 
     slot_table = dict(zip(offsets, slots_from))
 
@@ -203,12 +202,10 @@
         chunks.append(held)
     dense = put((0, 0), 0, kept_blocks, None)
     late = []
-    tie = [x_far, x_z, x_a]
+    tie = list(sends)
     for row, held in enumerate(chunks):
         names = list(held)
         tied = lax.optimization_barrier([held[name] for name in names] + tie + [dense])
-        if row == 0:
-            x_far, x_z, x_a = tied[-4:-1]
         dense = tied[-1]
         tie = []
         if row == 1 or rows_here == 1:
@@ -227,12 +224,12 @@
 
     half = column_blocks * BS // 2
     far = product(x_far).astype(jnp.bfloat16)
-    far, x_z, x_a = lax.optimization_barrier((far, x_z, x_a))
     far_first = swap(far[:, :half], sum_bit)
     far_second = swap(far[:, half:], sum_bit)
-    part_z = product(x_z)
-    part_z, x_a, x_own = lax.optimization_barrier((part_z, x_a, x_own))
-    part_a = product(x_a).astype(jnp.bfloat16)
+    far, x_z, x_a, x_own = lax.optimization_barrier((far, x_z, x_a, x_own))
+    both = product(jnp.concatenate([x_z, x_a], axis=0))
+    part_z = both[: x_z.shape[0]]
+    part_a = both[x_z.shape[0] :].astype(jnp.bfloat16)
     a_first = swap(part_a[:, :half], sum_bit)
     a_second = swap(part_a[:, half:], sum_bit)
     sum_first = (part_z[:, :half] + far_first.astype(jnp.float32)).astype(jnp.bfloat16)

time: 314 us -> 309 us (0.984)
  waiting for transfers between devices: 155 us -> 148 us
  other arithmetic: 16.8 us -> 21.6 us
    ppermute x21, waiting for transfers between devices: 154 us -> 147 us  [swap(): return lax.ppermute(value, ('dp', 'tensor'), pairs)]
    dot_general x4 -> x3, matrix products: 42.9 us -> 41.3 us  [product(): return jnp.dot(left, dense, preferred_element_type=jnp.float32)]
  transfers between devices with their start and end apart: 22 -> 22, of which waited for: 13 -> 9; matrix products, arithmetic and copies ran while one was open for 14% -> 23% of each run, Pallas kernels for 11% -> 12%
where the time goes in v5:
time: 309 us; the launch traced here: 308 us
  waiting for transfers between devices  148 us (48%)
  Pallas kernels  45.3 us (15%)
  matrix products  41.3 us (13%)
  starting transfers between devices  26.9 us (9%)
  other arithmetic  21.6 us (7%)
  between operations  13.7 us (4%)
  local copies, waits for them, and re-layouts  8.69 us (3%)
    ppermute x21, waiting for transfers between devices, swap(): return lax.ppermute(value, ('dp', 'tensor'), pairs)  147 us
    dot_general x3, matrix products, product(): return jnp.dot(left, dense, preferred_element_type=jnp.float32)  41.3 us
    pallas_call x10, Pallas kernels, place(): pl.pallas_call(functools.partial(place_body, slots=slots, column_blocks=c...  38 us
    ppermute x21, starting transfers between devices, swap(): return lax.ppermute(value, ('dp', 'tensor'), pairs)  26.9 us
    pallas_call x1, Pallas kernels, finish(): pl.pallas_call(functools.partial(finish_body, steps=steps, heads=heads),...  7.29 us
  transfers between devices with their start and end apart: 22, of which 9 were waited for; matrix products, arithmetic and copies ran while one was open for 23% of the time, Pallas kernels for 12%

profile of v5, /device:TPU:0, one launch (start us, length us, event | category | flops | bytes accessed | tf_op | source)
XLA Modules:
  0.0 307.5 jit_solution(6218217277964228147)
XLA Ops:
  6.5 0.7 all-gather.2.cloned.1.call-update
  7.3 0.7 iota_compare_fusion.1
  8.0 0.8 select_reduce_fusion
  8.8 4.1 %collective-permute-start.1 = (s32[4,40]{1,0:T(4,128)S(1)}, s32[4,40]{1,0:T(4,128)S(1)}, u32[]{:S(2)}, u32[]{:S(2)}) collective-permute-start(s32[4,40]{1,0:T(4,128)S(1)} %broadcast_add_fusion), channel_id=1, source_target_pairs={{0,16},{1,17},{2,18},{3,19},{4,20},{5,21},{6,22},{7,23},{8,24},{9,... | collective-permute-start | bytes 1928 | tf_op jit(solution)/shard_map/ppermute | solution.py:134
  12.9 1.5 collective-permute-start.2
  14.4 2.0 all_gather.7
  16.6 3.2 %collective-permute-done.3 = s32[4,40]{1,0:T(4,128)S(1)} collective-permute-done((s32[4,40]{1,0:T(4,128)S(1)}, s32[4,40]{1,0:T(4,128)S(1)}, u32[]{:S(2)}, u32[]{:S(2)}) %collective-permute-start.3) | collective-permute-done | bytes 672 | tf_op jit(solution)/shard_map/ppermute | solution.py:134
  19.8 0.5 collective-permute-start.9
  20.3 3.9 %fusion.13 = (bf16[128,3072]{1,0:T(8,128)(2,1)}, bf16[128,3072]{1,0:T(8,128)(2,1)}, bf16[128,3072]{1,0:T(8,128)(2,1)}, bf16[128,3072]{1,0:T(8,128)(2,1)}) fusion(bf16[512,3072]{1,0:T(8,128)(2,1)} %blocks_ref), kind=kLoop, calls=%fused_computation.68 | loop fusion | bytes 6291456 | tf_op jit(solution)/shard_map/slice | solution.py:197
  24.2 0.9 collective-permute-start.5
  25.1 2.1 collective-permute-start.6
  27.2 0.9 collective-permute-start.7
  28.1 0.6 pad_add_fusion.where_ref
  28.8 6.0 %shard_map.55.rest_0_ = bf16[2048,5120]{1,0:T(8,128)(2,1)} custom-call(s32[161]{0:T(256)} %pad_add_fusion.where_ref, bf16[512,3072]{1,0:T(8,128)(2,1)} %blocks_ref), custom_call_target="tpu_custom_call" | custom-call | bytes 8388608 | tf_op jit(solution)/shard_map/pallas_call | solution.py:41
  34.8 3.3 %fusion = f32[256]{0:T(256)S(1)} fusion(bf16[256,8192]{1,0:T(8,128)(2,1)} %all-gather.2.cloned.1.call-done), kind=kLoop, calls=%fused_computation.2 | loop fusion | flops 6291200 | bytes 4195328 | tf_op jit(solution)/shard_map/reduce_sum | solution.py:163
  38.3 1.2 fusion.2
  39.4 1.3 constant_dynamic-slice_fusion.3
  40.8 1.2 pad_maximum_fusion
  42.0 1.2 pad_maximum_fusion.1
  43.2 1.1 pad_maximum_fusion.2
  44.3 83.0 %collective-permute-done.7.blocks_ref = bf16[128,3072]{1,0:T(8,128)(2,1)} collective-permute-done((bf16[128,3072]{1,0:T(8,128)(2,1)}, bf16[128,3072]{1,0:T(8,128)(2,1)}, u32[]{:S(2)}, u32[]{:S(2)}) %collective-permute-start.7) | collective-permute-done | bytes 786464 | tf_op jit(solution)/shard_map/ppermute | solution.py:134
  127.2 1.5 collective-permute-start.8
  128.7 0.6 pad_add_fusion.5.where_ref
  129.4 3.2 %shard_map.56.rest_0_ = bf16[2048,5120]{1,0:T(8,128)(2,1)} custom-call(s32[41]{0:T(128)} %pad_add_fusion.5.where_ref, bf16[128,3072]{1,0:T(8,128)(2,1)} %collective-permute-done.7.blocks_ref, bf16[2048,5120]{1,0:T(8,128)(2,1)} %shard_map.55.rest_0_), custom_call_target="tpu_custom_call", output_to_operand_aliasing={{}: (2, {})} | custom-call | bytes 2097152 | tf_op jit(solution)/shard_map/pallas_call | solution.py:41
  132.6 0.5 collective-permute-start.10
  133.2 0.6 pad_add_fusion.3.where_ref
  133.8 0.6 pad_add_fusion.4.where_ref
  134.4 0.7 pad_add_fusion.6.where_ref
  135.1 0.6 pad_add_fusion.1.where_ref
  135.7 4.0 %collective-permute-start = (bf16[256,2048]{1,0:T(8,128)(2,1)}, bf16[256,2048]{1,0:T(8,128)(2,1)}, u32[]{:S(2)}, u32[]{:S(2)}) collective-permute-start(bf16[256,2048]{1,0:T(8,128)(2,1)} %pad_maximum_fusion), channel_id=1, source_target_pairs={{0,12},{1,11},{2,14},{3,9},{4,8},{5,15},{6,10},{7,13},{8,4},{9,3},... | collective-permute-start | bytes 3145736 | tf_op jit(solution)/shard_map/ppermute | solution.py:134
  139.6 0.6 pad_add_fusion.7.where_ref
  140.2 6.0 %shard_map.57.rest_0_ = bf16[2048,5120]{1,0:T(8,128)(2,1)} custom-call(s32[161]{0:T(256)} %pad_add_fusion.1.where_ref, bf16[512,3072]{1,0:T(8,128)(2,1)} %copy-done.1, bf16[2048,5120]{1,0:T(8,128)(2,1)} %shard_map.56.rest_0_), custom_call_target="tpu_custom_call", output_to_operand_aliasing={{}: (2, {})} | custom-call | bytes 8388608 | tf_op jit(solution)/shard_map/pallas_call | solution.py:41
  146.2 3.2 %shard_map.58.rest_0_ = bf16[2048,5120]{1,0:T(8,128)(2,1)} custom-call(s32[41]{0:T(128)} %pad_add_fusion.6.where_ref, bf16[128,3072]{1,0:T(8,128)(2,1)} %collective-permute-done.8.blocks_ref, bf16[2048,5120]{1,0:T(8,128)(2,1)} %shard_map.57.rest_0_), custom_call_target="tpu_custom_call", output_to_operand_aliasing={{}: (2, {})} | custom-call | bytes 2097152 | tf_op jit(solution)/shard_map/pallas_call | solution.py:41
  149.4 3.3 %shard_map.59.rest_0_ = bf16[2048,5120]{1,0:T(8,128)(2,1)} custom-call(s32[41]{0:T(128)} %pad_add_fusion.4.where_ref, bf16[128,3072]{1,0:T(8,128)(2,1)} %collective-permute-done.6.blocks_ref, bf16[2048,5120]{1,0:T(8,128)(2,1)} %shard_map.58.rest_0_), custom_call_target="tpu_custom_call", output_to_operand_aliasing={{}: (2, {})} | custom-call | bytes 2097152 | tf_op jit(solution)/shard_map/pallas_call | solution.py:41
  152.7 1.5 collective-permute-start.12
  154.2 1.4 collective-permute-done.10.blocks_ref
  155.6 3.3 %shard_map.60.rest_0_ = bf16[2048,5120]{1,0:T(8,128)(2,1)} custom-call(s32[41]{0:T(128)} %pad_add_fusion.7.where_ref, bf16[128,3072]{1,0:T(8,128)(2,1)} %collective-permute-done.10.blocks_ref, bf16[2048,5120]{1,0:T(8,128)(2,1)} %shard_map.59.rest_0_), custom_call_target="tpu_custom_call", output_to_operand_aliasing={{}: (2, {})} | custom-call | bytes 2097152 | tf_op jit(solution)/shard_map/pallas_call | solution.py:41
  158.8 3.3 %shard_map.61.rest_0_ = bf16[2048,5120]{1,0:T(8,128)(2,1)} custom-call(s32[41]{0:T(128)} %pad_add_fusion.3.where_ref, bf16[128,3072]{1,0:T(8,128)(2,1)} %collective-permute-done.5.blocks_ref, bf16[2048,5120]{1,0:T(8,128)(2,1)} %shard_map.60.rest_0_), custom_call_target="tpu_custom_call", output_to_operand_aliasing={{}: (2, {})} | custom-call | bytes 2097152 | tf_op jit(solution)/shard_map/pallas_call | solution.py:41
  162.2 6.9 %collective-permute-done.4.blocks_ref = bf16[128,3072]{1,0:T(8,128)(2,1)} collective-permute-done((bf16[128,3072]{1,0:T(8,128)(2,1)}, bf16[128,3072]{1,0:T(8,128)(2,1)}, u32[]{:S(2)}, u32[]{:S(2)}) %collective-permute-start.4) | collective-permute-done | bytes 786464 | tf_op jit(solution)/shard_map/ppermute | solution.py:134
  169.1 1.5 collective-permute-start.11
  171.3 0.6 pad_add_fusion.2.where_ref
  171.9 0.6 pad_add_fusion.8.where_ref
  172.4 0.7 pad_add_fusion.9.where_ref
  173.1 1.5 collective-permute-start.14
  174.6 1.2 pad_maximum_fusion.3
  175.8 3.2 %shard_map.62.rest_0_ = bf16[2048,5120]{1,0:T(8,128)(2,1)} custom-call(s32[41]{0:T(128)} %pad_add_fusion.9.where_ref, bf16[128,3072]{1,0:T(8,128)(2,1)} %collective-permute-done.12.blocks_ref, bf16[2048,5120]{1,0:T(8,128)(2,1)} %shard_map.61.rest_0_), custom_call_target="tpu_custom_call", output_to_operand_aliasing={{}: (2, {})} | custom-call | bytes 2097152 | tf_op jit(solution)/shard_map/pallas_call | solution.py:41
  179.0 3.2 %shard_map.63.rest_0_ = bf16[2048,5120]{1,0:T(8,128)(2,1)} custom-call(s32[41]{0:T(128)} %pad_add_fusion.8.where_ref, bf16[128,3072]{1,0:T(8,128)(2,1)} %collective-permute-done.4.blocks_ref, bf16[2048,5120]{1,0:T(8,128)(2,1)} %shard_map.62.rest_0_), custom_call_target="tpu_custom_call", output_to_operand_aliasing={{}: (2, {})} | custom-call | bytes 2097152 | tf_op jit(solution)/shard_map/pallas_call | solution.py:41
  182.3 8.7 %collective-permute-done.11.blocks_ref = bf16[128,3072]{1,0:T(8,128)(2,1)} collective-permute-done((bf16[128,3072]{1,0:T(8,128)(2,1)}, bf16[128,3072]{1,0:T(8,128)(2,1)}, u32[]{:S(2)}, u32[]{:S(2)}) %collective-permute-start.11) | collective-permute-done | bytes 786464 | tf_op jit(solution)/shard_map/ppermute | solution.py:134
  191.0 3.2 %shard_map.64 = bf16[2048,5120]{1,0:T(8,128)(2,1)} custom-call(s32[41]{0:T(128)} %pad_add_fusion.2.where_ref, bf16[128,3072]{1,0:T(8,128)(2,1)} %collective-permute-done.11.blocks_ref, bf16[2048,5120]{1,0:T(8,128)(2,1)} %shard_map.63.rest_0_), custom_call_target="tpu_custom_call", output_to_operand_aliasing={{}: (2, {})} | custom-call | bytes 2097152 | tf_op jit(solution)/shard_map/pallas_call | solution.py:41
  194.2 10.1 %convolution_convert_fusion = bf16[256,5120]{1,0:T(8,128)(2,1)S(1)} fusion(bf16[256,2048]{1,0:T(8,128)(2,1)} %collective-permute-done, bf16[2048,5120]{1,0:T(8,128)(2,1)} %shard_map.64), kind=kOutput, calls=%fused_computation.5 | convolution fusion | flops 5370019840 | bytes 24641536 | tf_op jit(solution)/shard_map/dot_general | solution.py:223
  204.6 1.0 copy-done.5
  205.6 2.1 collective-permute-start.17
  207.9 18.9 %fusion.15 = (bf16[512,5120]{1,0:T(8,128)(2,1)}, f32[512,5120]{1,0:T(8,128)}) fusion(bf16[2048,5120]{1,0:T(8,128)(2,1)} %shard_map.64, bf16[256,2048]{1,0:T(8,128)(2,1)} %copy-done.5, bf16[256,2048]{1,0:T(8,128)(2,1)} %copy-done.4), kind=kOutput, calls=%fused_computation.70 | convolution fusion | flops 10744233984 | bytes 38797312 | tf_op jit(solution)/shard_map/dot_general | solution.py:223
  226.8 1.9 fusion.12
  228.7 1.8 collective-permute-start.15
  230.8 2.0 fusion.4
  232.8 4.4 %collective-permute-done.18 = bf16[256,2560]{1,0:T(8,128)(2,1)S(1)} collective-permute-done((bf16[256,2560]{1,0:T(8,128)(2,1)S(1)}, bf16[256,2560]{1,0:T(8,128)(2,1)S(1)}, u32[]{:S(2)}, u32[]{:S(2)}) %collective-permute-start.18) | collective-permute-done | bytes 1310752 | tf_op jit(solution)/shard_map/ppermute | solution.py:134
  237.3 2.0 fusion.3
  239.3 2.1 collective-permute-start.20
  241.4 12.2 %fusion.16.own = f32[256,5120]{1,0:T(8,128)} fusion(bf16[256,2048]{1,0:T(8,128)(2,1)S(1)} %pad_maximum_fusion.3, bf16[2048,5120]{1,0:T(8,128)(2,1)} %shard_map.64), kind=kOutput, calls=%fused_computation.71 | convolution fusion | flops 5368709120 | bytes 27262976 | tf_op jit(solution)/shard_map/dot_general | solution.py:223
  253.6 11.8 %collective-permute-done.16.a_second = bf16[256,2560]{1,0:T(8,128)(2,1)S(1)} collective-permute-done((bf16[256,2560]{1,0:T(8,128)(2,1)S(1)}, bf16[256,2560]{1,0:T(8,128)(2,1)S(1)}, u32[]{:S(2)}, u32[]{:S(2)}) %collective-permute-start.16) | collective-permute-done | bytes 1310752 | tf_op jit(solution)/shard_map/ppermute | solution.py:134
  265.3 3.6 %collective-permute-done.19.z_first = bf16[256,2560]{1,0:T(8,128)(2,1)S(1)} collective-permute-done((bf16[256,2560]{1,0:T(8,128)(2,1)S(1)}, bf16[256,2560]{1,0:T(8,128)(2,1)S(1)}, u32[]{:S(2)}, u32[]{:S(2)}) %collective-permute-start.19) | collective-permute-done | bytes 1310752 | tf_op jit(solution)/shard_map/ppermute | solution.py:134
  269.0 24.4 %collective-permute-done.20.z_second = bf16[256,2560]{1,0:T(8,128)(2,1)S(1)} collective-permute-done((bf16[256,2560]{1,0:T(8,128)(2,1)S(1)}, bf16[256,2560]{1,0:T(8,128)(2,1)S(1)}, u32[]{:S(2)}, u32[]{:S(2)}) %collective-permute-start.20) | collective-permute-done | bytes 1310752 | tf_op jit(solution)/shard_map/ppermute | solution.py:134
  293.4 7.3 %shard_map.65 = bf16[256,5120]{1,0:T(8,128)(2,1)} custom-call(f32[256,5120]{1,0:T(8,128)} %fusion.16.own, bf16[256,2560]{1,0:T(8,128)(2,1)S(1)} %collective-permute-done.15.a_first, bf16[256,2560]{1,0:T(8,128)(2,1)S(1)} %collective-permute-done.16.a_second, bf16[256,2560]{1,0:T(8,128)(2,1)S(1)} %collective-permute-done.19.z_first, ...), custom_call_target="tpu_custom_call" | custom-call | flops 7864320 | bytes 13107200 | tf_op jit(solution)/shard_map/pallas_call | solution.py:100
  (43 shorter events, 1.9 us)
Async XLA Ops:
  6.5 28.3 %all-gather.2.cloned.1.call-start = ((), (), s32[]{:S(2)}) async-start(), calls=%async_computation | async-start | bytes 6291456 | tf_op jit(solution)/shard_map/all_gather | solution.py:159
  8.8 7.8 %collective-permute-start.1 = (s32[4,40]{1,0:T(4,128)S(1)}, s32[4,40]{1,0:T(4,128)S(1)}, u32[]{:S(2)}, u32[]{:S(2)}) collective-permute-start(s32[4,40]{1,0:T(4,128)S(1)} %broadcast_add_fusion), channel_id=1, source_target_pairs={{0,16},{1,17},{2,18},{3,19},{4,20},{5,21},{6,22},{7,23},{8,24},{9,... | collective-permute-start | bytes 1928 | tf_op jit(solution)/shard_map/ppermute | solution.py:134
  12.9 3.7 %collective-permute-start.2 = (s32[4,40]{1,0:T(4,128)S(1)}, s32[4,40]{1,0:T(4,128)S(1)}, u32[]{:S(2)}, u32[]{:S(2)}) collective-permute-start(s32[4,40]{1,0:T(4,128)S(1)} %broadcast_add_fusion), channel_id=1, source_target_pairs={{0,2},{1,5},{2,0},{3,7},{4,6},{5,1},{6,4},{7,3},{8,10},{9,13},{10,... | collective-permute-start | bytes 1928 | tf_op jit(solution)/shard_map/ppermute | solution.py:134
  14.4 5.4 %collective-permute-start.3 = (s32[4,40]{1,0:T(4,128)S(1)}, s32[4,40]{1,0:T(4,128)S(1)}, u32[]{:S(2)}, u32[]{:S(2)}) collective-permute-start(s32[4,40]{1,0:T(4,128)S(1)} %broadcast_add_fusion), channel_id=1, source_target_pairs={{0,18},{1,21},{2,16},{3,23},{4,22},{5,17},{6,20},{7,19},{8,26},{9,... | collective-permute-start | bytes 1928 | tf_op jit(solution)/shard_map/ppermute | solution.py:134
  19.8 115.9 %collective-permute-start.9 = (bf16[512,3072]{1,0:T(8,128)(2,1)}, bf16[512,3072]{1,0:T(8,128)(2,1)S(1)}, u32[]{:S(2)}, u32[]{:S(2)}) collective-permute-start(bf16[512,3072]{1,0:T(8,128)(2,1)} %blocks_ref), channel_id=1, source_target_pairs={{0,2},{1,5},{2,0},{3,7},{4,6},{5,1},{6,4},{7,3},{8,10},{9,13},{10,... | collective-permute-start | bytes 9437192 | tf_op jit(solution)/shard_map/ppermute | solution.py:134
  24.2 128.5 %collective-permute-start.5 = (bf16[128,3072]{1,0:T(8,128)(2,1)}, bf16[128,3072]{1,0:T(8,128)(2,1)}, u32[]{:S(2)}, u32[]{:S(2)}) collective-permute-start(bf16[128,3072]{1,0:T(8,128)(2,1)} %get-tuple-element.61), channel_id=1, source_target_pairs={{0,16},{1,17},{2,18},{3,19},{4,20},{5,21},{6,22},{7,23},{8,24},{9,... | collective-permute-start | bytes 2359304 | tf_op jit(solution)/shard_map/ppermute | solution.py:134
  25.1 107.4 %collective-permute-start.6 = (bf16[128,3072]{1,0:T(8,128)(2,1)}, bf16[128,3072]{1,0:T(8,128)(2,1)}, u32[]{:S(2)}, u32[]{:S(2)}) collective-permute-start(bf16[128,3072]{1,0:T(8,128)(2,1)} %get-tuple-element.60), channel_id=1, source_target_pairs={{0,16},{1,17},{2,18},{3,19},{4,20},{5,21},{6,22},{7,23},{8,24},{9,... | collective-permute-start | bytes 2359304 | tf_op jit(solution)/shard_map/ppermute | solution.py:134
  27.2 100.0 %collective-permute-start.7 = (bf16[128,3072]{1,0:T(8,128)(2,1)}, bf16[128,3072]{1,0:T(8,128)(2,1)}, u32[]{:S(2)}, u32[]{:S(2)}) collective-permute-start(bf16[128,3072]{1,0:T(8,128)(2,1)} %get-tuple-element.59), channel_id=1, source_target_pairs={{0,16},{1,17},{2,18},{3,19},{4,20},{5,21},{6,22},{7,23},{8,24},{9,... | collective-permute-start | bytes 2359304 | tf_op jit(solution)/shard_map/ppermute | solution.py:134
  34.8 3.5 %copy-start = (bf16[256,8192]{1,0:T(8,128)(2,1)S(1)}, bf16[256,8192]{1,0:T(8,128)(2,1)}, u32[]{:S(2)}) copy-start(bf16[256,8192]{1,0:T(8,128)(2,1)} %all-gather.2.cloned.1.call-done) | copy-start | bytes 12582916
  127.2 19.0 %collective-permute-start.8 = (bf16[128,3072]{1,0:T(8,128)(2,1)}, bf16[128,3072]{1,0:T(8,128)(2,1)}, u32[]{:S(2)}, u32[]{:S(2)}) collective-permute-start(bf16[128,3072]{1,0:T(8,128)(2,1)} %collective-permute-done.7.blocks_ref), channel_id=1, source_target_pairs={{0,2},{1,5},{2,0},{3,7},{4,6},{5,1},{6,4},{7,3},{8,10},{9,13},{10,... | collective-permute-start | bytes 2359304 | tf_op jit(solution)/shard_map/ppermute | solution.py:134
  132.6 23.0 %collective-permute-start.10 = (bf16[128,3072]{1,0:T(8,128)(2,1)}, bf16[128,3072]{1,0:T(8,128)(2,1)}, u32[]{:S(2)}, u32[]{:S(2)}) collective-permute-start(bf16[128,3072]{1,0:T(8,128)(2,1)} %collective-permute-done.6.blocks_ref), channel_id=1, source_target_pairs={{0,2},{1,5},{2,0},{3,7},{4,6},{5,1},{6,4},{7,3},{8,10},{9,13},{10,... | collective-permute-start | bytes 2359304 | tf_op jit(solution)/shard_map/ppermute | solution.py:134
  133.1 36.0 %collective-permute-start.4 = (bf16[128,3072]{1,0:T(8,128)(2,1)}, bf16[128,3072]{1,0:T(8,128)(2,1)}, u32[]{:S(2)}, u32[]{:S(2)}) collective-permute-start(bf16[128,3072]{1,0:T(8,128)(2,1)} %get-tuple-element.62), channel_id=1, source_target_pairs={{0,16},{1,17},{2,18},{3,19},{4,20},{5,21},{6,22},{7,23},{8,24},{9,... | collective-permute-start | bytes 2359304 | tf_op jit(solution)/shard_map/ppermute | solution.py:134
  135.7 4.5 %copy-start.1 = (bf16[512,3072]{1,0:T(8,128)(2,1)}, bf16[512,3072]{1,0:T(8,128)(2,1)S(1)}, u32[]{:S(2)}) copy-start(bf16[512,3072]{1,0:T(8,128)(2,1)S(1)} %collective-permute-done.9.blocks_ref) | copy-start | bytes 9437188
  135.7 58.5 %collective-permute-start = (bf16[256,2048]{1,0:T(8,128)(2,1)}, bf16[256,2048]{1,0:T(8,128)(2,1)}, u32[]{:S(2)}, u32[]{:S(2)}) collective-permute-start(bf16[256,2048]{1,0:T(8,128)(2,1)} %pad_maximum_fusion), channel_id=1, source_target_pairs={{0,12},{1,11},{2,14},{3,9},{4,8},{5,15},{6,10},{7,13},{8,4},{9,3},... | collective-permute-start | bytes 3145736 | tf_op jit(solution)/shard_map/ppermute | solution.py:134
  152.7 23.1 %collective-permute-start.12 = (bf16[128,3072]{1,0:T(8,128)(2,1)}, bf16[128,3072]{1,0:T(8,128)(2,1)}, u32[]{:S(2)}, u32[]{:S(2)}) collective-permute-start(bf16[128,3072]{1,0:T(8,128)(2,1)} %collective-permute-done.5.blocks_ref), channel_id=1, source_target_pairs={{0,2},{1,5},{2,0},{3,7},{4,6},{5,1},{6,4},{7,3},{8,10},{9,13},{10,... | collective-permute-start | bytes 2359304 | tf_op jit(solution)/shard_map/ppermute | solution.py:134
  158.8 14.2 %copy-start.2 = (bf16[256,2048]{1,0:T(8,128)(2,1)S(1)}, bf16[256,2048]{1,0:T(8,128)(2,1)}, u32[]{:S(2)}) copy-start(bf16[256,2048]{1,0:T(8,128)(2,1)} %pad_maximum_fusion.1) | copy-start | bytes 3145732
  158.8 14.2 %copy-start.3 = (bf16[256,2048]{1,0:T(8,128)(2,1)S(1)}, bf16[256,2048]{1,0:T(8,128)(2,1)}, u32[]{:S(2)}) copy-start(bf16[256,2048]{1,0:T(8,128)(2,1)} %pad_maximum_fusion.2) | copy-start | bytes 3145732
  169.1 21.9 %collective-permute-start.11 = (bf16[128,3072]{1,0:T(8,128)(2,1)}, bf16[128,3072]{1,0:T(8,128)(2,1)}, u32[]{:S(2)}, u32[]{:S(2)}) collective-permute-start(bf16[128,3072]{1,0:T(8,128)(2,1)} %collective-permute-done.4.blocks_ref), channel_id=1, source_target_pairs={{0,2},{1,5},{2,0},{3,7},{4,6},{5,1},{6,4},{7,3},{8,10},{9,13},{10,... | collective-permute-start | bytes 2359304 | tf_op jit(solution)/shard_map/ppermute | solution.py:134
  173.1 31.4 %collective-permute-start.13 = (bf16[256,2048]{1,0:T(8,128)(2,1)S(1)}, bf16[256,2048]{1,0:T(8,128)(2,1)S(1)}, u32[]{:S(2)}, u32[]{:S(2)}) collective-permute-start(bf16[256,2048]{1,0:T(8,128)(2,1)S(1)} %copy-done.2), channel_id=1, source_target_pairs={{0,8},{1,9},{2,10},{3,11},{4,12},{5,13},{6,14},{7,15},{8,0},{9,1},... | collective-permute-start | bytes 3145736 | tf_op jit(solution)/shard_map/ppermute | solution.py:134
  173.1 31.5 %collective-permute-start.14 = (bf16[256,2048]{1,0:T(8,128)(2,1)S(1)}, bf16[256,2048]{1,0:T(8,128)(2,1)S(1)}, u32[]{:S(2)}, u32[]{:S(2)}) collective-permute-start(bf16[256,2048]{1,0:T(8,128)(2,1)S(1)} %copy-done.3), channel_id=1, source_target_pairs={{0,4},{1,3},{2,6},{3,1},{4,0},{5,7},{6,2},{7,5},{8,12},{9,11},{10,... | collective-permute-start | bytes 3145736 | tf_op jit(solution)/shard_map/ppermute | solution.py:134
  204.5 3.1 %copy-start.4 = (bf16[256,2048]{1,0:T(8,128)(2,1)}, bf16[256,2048]{1,0:T(8,128)(2,1)S(1)}, u32[]{:S(2)}) copy-start(bf16[256,2048]{1,0:T(8,128)(2,1)S(1)} %collective-permute-done.13) | copy-start | bytes 3145732
  204.6 1.0 copy-start.5
  205.6 25.2 %collective-permute-start.17 = (bf16[256,2560]{1,0:T(8,128)(2,1)S(1)}, bf16[256,2560]{1,0:T(8,128)(2,1)S(1)}, u32[]{:S(2)}, u32[]{:S(2)}) collective-permute-start(bf16[256,2560]{1,0:T(8,128)(2,1)S(1)} %get-tuple-element.64), channel_id=1, source_target_pairs={{0,4},{1,3},{2,6},{3,1},{4,0},{5,7},{6,2},{7,5},{8,12},{9,11},{10,... | collective-permute-start | bytes 3932168 | tf_op jit(solution)/shard_map/ppermute | solution.py:134
  207.6 29.6 %collective-permute-start.18 = (bf16[256,2560]{1,0:T(8,128)(2,1)S(1)}, bf16[256,2560]{1,0:T(8,128)(2,1)S(1)}, u32[]{:S(2)}, u32[]{:S(2)}) collective-permute-start(bf16[256,2560]{1,0:T(8,128)(2,1)S(1)} %get-tuple-element.63), channel_id=1, source_target_pairs={{0,4},{1,3},{2,6},{3,1},{4,0},{5,7},{6,2},{7,5},{8,12},{9,11},{10,... | collective-permute-start | bytes 3932168 | tf_op jit(solution)/shard_map/ppermute | solution.py:134
  228.7 24.9 %collective-permute-start.15 = (bf16[256,2560]{1,0:T(8,128)(2,1)S(1)}, bf16[256,2560]{1,0:T(8,128)(2,1)S(1)}, u32[]{:S(2)}, u32[]{:S(2)}) collective-permute-start(bf16[256,2560]{1,0:T(8,128)(2,1)S(1)} %get-tuple-element.42), channel_id=1, source_target_pairs={{0,4},{1,3},{2,6},{3,1},{4,0},{5,7},{6,2},{7,5},{8,12},{9,11},{10,... | collective-permute-start | bytes 3932168 | tf_op jit(solution)/shard_map/ppermute | solution.py:134
  230.5 34.8 %collective-permute-start.16 = (bf16[256,2560]{1,0:T(8,128)(2,1)S(1)}, bf16[256,2560]{1,0:T(8,128)(2,1)S(1)}, u32[]{:S(2)}, u32[]{:S(2)}) collective-permute-start(bf16[256,2560]{1,0:T(8,128)(2,1)S(1)} %get-tuple-element.41), channel_id=1, source_target_pairs={{0,4},{1,3},{2,6},{3,1},{4,0},{5,7},{6,2},{7,5},{8,12},{9,11},{10,... | collective-permute-start | bytes 3932168 | tf_op jit(solution)/shard_map/ppermute | solution.py:134
  237.3 31.7 %collective-permute-start.19 = (bf16[256,2560]{1,0:T(8,128)(2,1)S(1)}, bf16[256,2560]{1,0:T(8,128)(2,1)S(1)}, u32[]{:S(2)}, u32[]{:S(2)}) collective-permute-start(bf16[256,2560]{1,0:T(8,128)(2,1)S(1)} %fusion.4), channel_id=1, source_target_pairs={{0,8},{1,9},{2,10},{3,11},{4,12},{5,13},{6,14},{7,15},{8,0},{9,1},... | collective-permute-start | bytes 3932168 | tf_op jit(solution)/shard_map/ppermute | solution.py:134
  239.3 54.1 %collective-permute-start.20 = (bf16[256,2560]{1,0:T(8,128)(2,1)S(1)}, bf16[256,2560]{1,0:T(8,128)(2,1)S(1)}, u32[]{:S(2)}, u32[]{:S(2)}) collective-permute-start(bf16[256,2560]{1,0:T(8,128)(2,1)S(1)} %fusion.3), channel_id=1, source_target_pairs={{0,8},{1,9},{2,10},{3,11},{4,12},{5,13},{6,14},{7,15},{8,0},{9,1},... | collective-permute-start | bytes 3932168 | tf_op jit(solution)/shard_map/ppermute | solution.py:134
Sparse Core Ops, SparseCore 0:
  8.9 16.3 all-gather.1
